TPU v7x, 32 devices: a whole 2x2x4 slice. The times are simulated.
32 devices in a mesh: leaf: 16 (over z, y, x), head: 2 (over core).
Axes of the slice: x: 2, y: 2, z: 4, core: 2. Of those that a mesh axis runs over, the one named last changes fastest.
Arguments:
- cand_owner: int32 [128, 500, 1], P('leaf'), may hold values from 0 to 15; in each aligned block of 4000 rows (0 to 3999, 4000 to 7999, ..., all dimensions but the last counted through in order) at most 500 rows name the same one
- cand_row: int32 [128, 500], P('leaf'), may hold values from 0 to 2047
- table: bfloat16 [32768, 1024], P('leaf', 'head'), may hold values from -6 to 6
- position: bfloat16 [500, 1024], P(None, 'head'), may hold values from -3 to 3
- w_query: bfloat16 [1024, 1024], P(None, 'head'), may hold values from -0.375 to 0.375
- w_key: bfloat16 [1024, 1024], P(None, 'head'), may hold values from -0.375 to 0.375
- w_value: bfloat16 [1024, 1024], P(None, 'head'), may hold values from -0.1875 to 0.1875
- w_out: bfloat16 [1024, 1024], P('head'), may hold values from -0.1875 to 0.1875
- gain: float32 [1024], P('head'), may hold values from 0.1 to 1.9
- shift_bias: float32 [1024], P('head'), may hold values from -3 to 3
Outputs:
- reranked: bfloat16 [128, 500, 1024], P('leaf', None, 'head')
Inputs may be any that keep to these rules, and one draw needn't show every extreme that they name: `cand_owner`: among the 4000 candidates of the lists of one index of leaf, no subtree is named more than 500 times, a bound that some block reaches.
All inputs are finite; a program needn't handle non-finite values.
Results may differ from a plain program's by a relative error of at most 0.012.
Values may be sent and summed in bfloat16 or wider, within the bound.
A program may use at most 128 MiB of HBM per device.

v0:
```python
import jax
import jax.numpy as jnp
from jax import lax
from jax.sharding import PartitionSpec as P

HEAD_DIM = 64


def arrange_weights(query_w, key_w, value_w):
    rows, width = query_w.shape
    heads_local = width // HEAD_DIM
    stacked = jnp.stack(
        (
            query_w.reshape(rows, heads_local, HEAD_DIM),
            key_w.reshape(rows, heads_local, HEAD_DIM),
            value_w.reshape(rows, heads_local, HEAD_DIM),
        ),
        axis=2,
    )
    return stacked.reshape(rows, heads_local, 3 * HEAD_DIM)


def project_heads(weight_rows, rows3):
    return lax.dot_general(
        weight_rows, rows3, (((0,), (2,)), ((), ())), preferred_element_type=jnp.float32
    )


def attend_heads(qkv_t):
    heads_local, _, users, length = qkv_t.shape
    scale = 1.0 / HEAD_DIM**0.5

    def one_user(index, result):
        part = lax.dynamic_index_in_dim(qkv_t, index, 2, keepdims=False)
        query = part[:, :HEAD_DIM]
        keys = part[:, HEAD_DIM : 2 * HEAD_DIM]
        values = part[:, 2 * HEAD_DIM :]
        scores = (
            lax.dot_general(
                query, keys, (((1,), (1,)), ((0,), (0,))), preferred_element_type=jnp.float32
            )
            * scale
        )
        weights = jax.nn.softmax(scores, axis=-1).astype(jnp.bfloat16)
        context = lax.dot_general(
            values, weights, (((2,), (2,)), ((0,), (0,))), preferred_element_type=jnp.float32
        )
        return lax.dynamic_update_index_in_dim(result, context.astype(jnp.bfloat16), index, 0)

    start = jnp.zeros((users, heads_local, HEAD_DIM, length), jnp.bfloat16)
    return lax.fori_loop(0, users, one_user, start)


def mix_heads(context, out_heads):
    return lax.dot_general(
        context, out_heads, (((1, 2), (0, 1)), ((), ())), preferred_element_type=jnp.float32
    )


def shards(cand_owner, cand_row, table, position, w_query, w_key, w_value, w_out, gain, shift_bias):
    users, length, _ = cand_owner.shape
    total = users * length
    cols = table.shape[1]
    n_leaf = lax.axis_size("leaf")
    n_head = lax.axis_size("head")
    capacity = max(2, 2 * total // n_leaf)
    owner = cand_owner.reshape(total)
    local_row = cand_row.reshape(total)
    onehot = (owner[:, None] == jnp.arange(n_leaf, dtype=jnp.int32)[None, :]).astype(jnp.int32)
    earlier = jnp.cumsum(onehot, axis=0) - onehot
    rank = jnp.sum(earlier * onehot, axis=1)
    target = owner * capacity + rank
    requests = (
        jnp.zeros((n_leaf * capacity,), jnp.int32)
        .at[target]
        .set(local_row)
        .reshape(n_leaf, capacity)
    )
    found = jnp.take(
        table, lax.all_to_all(requests, "leaf", split_axis=0, concat_axis=0, tiled=True), axis=0
    )
    fetched = lax.all_to_all(found, "leaf", split_axis=0, concat_axis=0, tiled=True)
    embedded = jnp.take(fetched.reshape(n_leaf * capacity, cols), target, axis=0)
    summed = (
        embedded.astype(jnp.float32).reshape(users, length, cols)
        + position.astype(jnp.float32)[None]
    )
    x = summed.astype(jnp.bfloat16).reshape(total, cols)
    full_query, full_key, full_value, full_out = (
        lax.all_gather(w_query, "head", axis=1, tiled=True),
        lax.all_gather(w_key, "head", axis=1, tiled=True),
        lax.all_gather(w_value, "head", axis=1, tiled=True),
        lax.all_gather(w_out, "head", axis=0, tiled=True),
    )
    full_gain, full_bias = (
        lax.all_gather(gain, "head", axis=0, tiled=True),
        lax.all_gather(shift_bias, "head", axis=0, tiled=True),
    )
    user_rows = lax.all_to_all(x, "head", split_axis=0, concat_axis=1, tiled=True)
    own_users = users // n_head
    width = user_rows.shape[1]
    rows3 = user_rows.reshape(own_users, length, width)
    joined = arrange_weights(full_query, full_key, full_value)
    qkv_t = project_heads(joined, rows3).astype(jnp.bfloat16)
    context = attend_heads(qkv_t)
    out_heads = full_out.reshape(width // HEAD_DIM, HEAD_DIM, width)
    y = rows3.astype(jnp.float32) + mix_heads(context, out_heads)
    mean = jnp.mean(y, axis=2, keepdims=True)
    var = jnp.mean(y * y, axis=2, keepdims=True) - mean * mean
    normed = (y - mean) * lax.rsqrt(var + 1e-05) * full_gain[None, None, :] + full_bias[
        None, None, :
    ]
    normed_rows = normed.astype(jnp.bfloat16).reshape(own_users * length, width)
    reranked = lax.all_to_all(normed_rows, "head", split_axis=1, concat_axis=0, tiled=True)
    return reranked.reshape(users, length, cols)


def solution(mesh):
    return jax.shard_map(
        shards,
        mesh=mesh,
        in_specs=(
            P("leaf", None, None),
            P("leaf", None),
            P("leaf", "head"),
            P(None, "head"),
            P(None, "head"),
            P(None, "head"),
            P(None, "head"),
            P("head", None),
            P("head"),
            P("head"),
        ),
        out_specs=P("leaf", None, "head"),
        check_vma=False,
    )
```

profile of v0, /device:TPU:29, one launch (start us, length us, event | category | flops | bytes accessed | tf_op | source)
XLA Modules:
  0.0 506.7 jit_solution(11365379484532144303)
XLA Ops:
  14.3 19.3 %scatter_custom_fusion = s32[8000]{0:T(1024)S(1)} fusion(s32[4000]{0:T(1024)S(1)} %bitcast.65, s32[4000]{0:T(1024)S(1)} %reshape.185, s32[]{:T(128)} %copy.49), kind=kCustom, calls=%fused_computation.48 | custom fusion | bytes 32004 | tf_op jit(solution)/shard_map/scatter | solution.py:76
  33.8 8.9 %all_to_all.49 = s32[16,1,500]{2,1,0:T(1,128)S(1)} all-to-all(s32[16,1,500]{2,1,0:T(1,128)S(1)} %all_to_all.35), channel_id=1, replica_groups=mesh['leaf'=16,'head'=2] {'leaf'}, dimensions={0} | all-to-all | bytes 64000 | tf_op jit(solution)/shard_map/all_to_all | solution.py:80
  42.9 23.5 %gather_fusion = bf16[8000,512]{1,0:T(8,128)(2,1)} fusion(bf16[2048,512]{1,0:T(8,128)(2,1)S(1)} %copy-done, s32[8192]{0:T(1024)S(1)} %pad_clamp_fusion), kind=kCustom, calls=%fused_computation | custom fusion | bytes 16416000 | tf_op jit(solution)/shard_map/jit(_take)/gather | solution.py:79
  66.4 9.3 %reshape.166 = bf16[16,500,512]{2,1,0:T(8,128)(2,1)} reshape(bf16[8000,512]{1,0:T(8,128)(2,1)} %gather_fusion) | data formatting | bytes 16384000 | tf_op jit(solution)/shard_map/jit(_take)/gather | solution.py:79
  75.7 7.3 %broadcast_select_fusion = bf16[16,500,512]{2,1,0:T(8,128)(2,1)} fusion(bf16[16,500,512]{2,1,0:T(8,128)(2,1)} %reshape.166, pred[16,500]{1,0:T(8,128)(4,1)S(1)} %compare_and_fusion), kind=kLoop, calls=%fused_computation.25 | loop fusion | flops 4096000 | bytes 16392000 | tf_op jit(solution)/shard_map/jit(_take)/select_n | solution.py:79
  83.1 8.3 %all-to-all-start.1 = ((bf16[16,500,512]{2,1,0:T(8,128)(2,1)}), bf16[16,500,512]{2,1,0:T(8,128)(2,1)}, u32[]{:S(2)}, u32[]{:S(2)}) async-start(bf16[16,500,512]{2,1,0:T(8,128)(2,1)} %broadcast_select_fusion), calls=%async_computation.1 | async-start | bytes 16515072 | tf_op jit(solution)/shard_map/all_to_all | solution.py:82
  100.7 7.3 %add.129 = f32[2,2000,512]{2,1,0:T(8,128)} reshape(f32[8,500,512]{2,1,0:T(8,128)} %add.128) | data formatting | bytes 16384000 | tf_op jit(solution)/shard_map/add | solution.py:85
  114.0 7.0 %all-gather.7.cloned.1.call-done = bf16[1024,1024]{0,1:T(8,128)(2,1)} async-done(((bf16[1024,512]{0,1:T(8,128)(2,1)}), bf16[1024,1024]{0,1:T(8,128)(2,1)}) %all-gather.7.cloned.1.call-update) | async-done | bytes 2097168 | tf_op jit(solution)/shard_map/all_gather | solution.py:90
  121.1 13.3 %all-gather.9.cloned.1.call-done = bf16[1024,1024]{0,1:T(8,128)(2,1)} async-done(((bf16[1024,512]{0,1:T(8,128)(2,1)}), bf16[1024,1024]{0,1:T(8,128)(2,1)}) %all-gather.9.cloned.1.call-update) | async-done | bytes 2097168 | tf_op jit(solution)/shard_map/all_gather | solution.py:91
  141.3 133.3 %all-to-all-done.1 = bf16[16,500,512]{2,1,0:T(8,128)(2,1)} async-done(((bf16[16,500,512]{2,1,0:T(8,128)(2,1)}), bf16[16,500,512]{2,1,0:T(8,128)(2,1)}, u32[]{:S(2)}, u32[]{:S(2)}) %all-to-all-start.1) | async-done | bytes 8192032 | tf_op jit(solution)/shard_map/all_to_all | solution.py:82
  274.7 9.3 %reshape.159 = bf16[8000,512]{1,0:T(8,128)(2,1)} reshape(bf16[16,500,512]{2,1,0:T(8,128)(2,1)} %all-to-all-done.1) | data formatting | bytes 16384000 | tf_op jit(solution)/shard_map/reshape | solution.py:83
  284.0 21.8 %gather_fusion.1 = bf16[4000,512]{1,0:T(8,128)(2,1)} fusion(bf16[8000,512]{1,0:T(8,128)(2,1)} %reshape.159, s32[4096]{0:T(1024)S(1)} %pad_clamp_fusion.1), kind=kCustom, calls=%fused_computation.1 | custom fusion | bytes 8208000 | tf_op jit(solution)/shard_map/jit(_take)/gather | solution.py:83
  305.8 5.2 %add_convert_fusion.1 = bf16[2,2000,512]{2,1,0:T(8,128)(2,1)S(1)} fusion(f32[2,2000,512]{2,1,0:T(8,128)} %add.129, bf16[2,2000,512]{2,1,0:T(8,128)(2,1)} %bitcast.54, pred[2,2000]{1,0:T(4,128)(4,1)S(1)} %compare_and_fusion.1), kind=kLoop, calls=%fused_computation.26 | loop fusion | flops 8192000 | bytes 16388000 | tf_op jit(solution)/shard_map/convert_element_type | solution.py:88
  311.1 9.7 %all_to_all.50 = bf16[2,2000,512]{2,1,0:T(8,128)(2,1)S(1)} all-to-all(bf16[2,2000,512]{2,1,0:T(8,128)(2,1)S(1)} %add_convert_fusion.1), channel_id=1, replica_groups=mesh['leaf'=16,'head'=2] {'head'}, dimensions={0} | all-to-all | bytes 8192000 | tf_op jit(solution)/shard_map/all_to_all | solution.py:99
  320.8 18.6 %copy.23 = bf16[2000,2,512]{2,1,0:T(2,128)(2,1)} copy(bf16[2000,2,512]{2,0,1:T(8,128)(2,1)S(1)} %bitcast.55) | data formatting | bytes 8192000 | tf_op jit(solution)/shard_map/all_to_all | solution.py:99
  339.4 5.8 %reshape.195 = bf16[4,500,1024,1]{2,1,0,3:T(8,128)(2,1)} reshape(bf16[2000,2,512]{2,1,0:T(2,128)(2,1)} %copy.23) | data formatting | bytes 8192000 | tf_op jit(solution)/shard_map/reshape | solution.py:102
  345.1 19.3 %convolution_convert_fusion = bf16[16,192,4,500]{3,1,0,2:T(8,128)(2,1)} fusion(bf16[1024,16,192,1]{0,2,1,3:T(8,128)(2,1)} %bitcast.57, bf16[4,500,1024,1]{2,1,0,3:T(8,128)(2,1)} %reshape.195), kind=kOutput, calls=%fused_computation.27 | convolution fusion | flops 12589056000 | bytes 22675456 | tf_op jit(solution)/shard_map/dot_general | solution.py:24
  364.4 90.3 %while.13 = (s32[]{:T(128)}, bf16[4,16,64,500]{3,2,1,0:T(8,128)(2,1)}, bf16[16,192,4,500]{3,1,0,2:T(8,128)(2,1)}, s32[]{:T(128)}) while((s32[]{:T(128)}, bf16[4,16,64,500]{3,2,1,0:T(8,128)(2,1)}, bf16[16,192,4,500]{3,1,0,2:T(8,128)(2,1)}, s32[]{:T(128)}) %tuple.35), condition=%wide.region_7.8_spmd, body=%wide.region_4.7_spmd.sunk | while | flops 1044512512 | bytes 42917944 | solution.py:51
  368.2 10.0 %fusion.52 = (f32[16,500]{1,0:T(8,128)S(1)}, f32[16,500,500]{1,2,0:T(8,128)}) fusion(bf16[16,192,500]{2,1,0:T(8,128)(2,1)} %dynamic-slice_bitcast_fusion.2), kind=kOutput, calls=%fused_computation.55.clone.1 | convolution fusion | flops 524000512 | bytes 18129152 | tf_op jit(solution)/shard_map/while/body/eval_jaxpr/sub | solution.py:44
  378.2 8.7 %fusion.53 = bf16[4,16,64,500]{3,2,1,0:T(8,128)(2,1)} fusion(bf16[4,16,64,500]{3,2,1,0:T(8,128)(2,1)} %get-tuple-element.113, s32[]{:T(128)} %get-tuple-element.112, f32[16,500,500]{1,2,0:T(8,128)} %get-tuple-element.106, f32[16,500]{1,0:T(8,128)S(1)} %get-tuple-element.107, bf16[16,192,500]{2,1,0:T(8,128)(2,1)} %dynamic-slice_bitcast_fusion.2), kind=kOutput, calls=%fused_computation.14.clone.1 | convolution fusion | flops 520512000 | bytes 18644736 | tf_op jit(solution)/shard_map/while/body/eval_jaxpr/dot_general | solution.py:45
  390.8 9.9 %fusion.52 = (f32[16,500]{1,0:T(8,128)S(1)}, f32[16,500,500]{1,2,0:T(8,128)}) fusion(bf16[16,192,500]{2,1,0:T(8,128)(2,1)} %dynamic-slice_bitcast_fusion.2), kind=kOutput, calls=%fused_computation.55.clone.1 | convolution fusion | flops 524000512 | bytes 18129152 | tf_op jit(solution)/shard_map/while/body/eval_jaxpr/sub | solution.py:44
  400.7 8.7 %fusion.53 = bf16[4,16,64,500]{3,2,1,0:T(8,128)(2,1)} fusion(bf16[4,16,64,500]{3,2,1,0:T(8,128)(2,1)} %get-tuple-element.113, s32[]{:T(128)} %get-tuple-element.112, f32[16,500,500]{1,2,0:T(8,128)} %get-tuple-element.106, f32[16,500]{1,0:T(8,128)S(1)} %get-tuple-element.107, bf16[16,192,500]{2,1,0:T(8,128)(2,1)} %dynamic-slice_bitcast_fusion.2), kind=kOutput, calls=%fused_computation.14.clone.1 | convolution fusion | flops 520512000 | bytes 18644736 | tf_op jit(solution)/shard_map/while/body/eval_jaxpr/dot_general | solution.py:45
  413.3 10.0 %fusion.52 = (f32[16,500]{1,0:T(8,128)S(1)}, f32[16,500,500]{1,2,0:T(8,128)}) fusion(bf16[16,192,500]{2,1,0:T(8,128)(2,1)} %dynamic-slice_bitcast_fusion.2), kind=kOutput, calls=%fused_computation.55.clone.1 | convolution fusion | flops 524000512 | bytes 18129152 | tf_op jit(solution)/shard_map/while/body/eval_jaxpr/sub | solution.py:44
  423.3 8.8 %fusion.53 = bf16[4,16,64,500]{3,2,1,0:T(8,128)(2,1)} fusion(bf16[4,16,64,500]{3,2,1,0:T(8,128)(2,1)} %get-tuple-element.113, s32[]{:T(128)} %get-tuple-element.112, f32[16,500,500]{1,2,0:T(8,128)} %get-tuple-element.106, f32[16,500]{1,0:T(8,128)S(1)} %get-tuple-element.107, bf16[16,192,500]{2,1,0:T(8,128)(2,1)} %dynamic-slice_bitcast_fusion.2), kind=kOutput, calls=%fused_computation.14.clone.1 | convolution fusion | flops 520512000 | bytes 18644736 | tf_op jit(solution)/shard_map/while/body/eval_jaxpr/dot_general | solution.py:45
  435.9 10.0 %fusion.52 = (f32[16,500]{1,0:T(8,128)S(1)}, f32[16,500,500]{1,2,0:T(8,128)}) fusion(bf16[16,192,500]{2,1,0:T(8,128)(2,1)} %dynamic-slice_bitcast_fusion.2), kind=kOutput, calls=%fused_computation.55.clone.1 | convolution fusion | flops 524000512 | bytes 18129152 | tf_op jit(solution)/shard_map/while/body/eval_jaxpr/sub | solution.py:44
  445.9 8.8 %fusion.53 = bf16[4,16,64,500]{3,2,1,0:T(8,128)(2,1)} fusion(bf16[4,16,64,500]{3,2,1,0:T(8,128)(2,1)} %get-tuple-element.113, s32[]{:T(128)} %get-tuple-element.112, f32[16,500,500]{1,2,0:T(8,128)} %get-tuple-element.106, f32[16,500]{1,0:T(8,128)S(1)} %get-tuple-element.107, bf16[16,192,500]{2,1,0:T(8,128)(2,1)} %dynamic-slice_bitcast_fusion.2), kind=kOutput, calls=%fused_computation.14.clone.1 | convolution fusion | flops 520512000 | bytes 18644736 | tf_op jit(solution)/shard_map/while/body/eval_jaxpr/dot_general | solution.py:45
  454.7 5.8 %reshape.160 = bf16[4,500,1024]{2,1,0:T(8,128)(2,1)} reshape(bf16[2000,2,512]{2,1,0:T(2,128)(2,1)} %copy.23) | data formatting | bytes 8192000 | tf_op jit(solution)/shard_map/reshape | solution.py:102
  460.4 9.9 %fusion.30 = (f32[4,500]{1,0:T(4,128)S(1)}, f32[4,500]{1,0:T(4,128)S(1)}, f32[4,500,1024]{2,1,0:T(8,128)S(1)}) fusion(bf16[4,16,64,500]{3,2,1,0:T(8,128)(2,1)} %get-tuple-element.69, bf16[16,64,1024,1]{2,1,0,3:T(8,128)(2,1)} %bitcast.72, bf16[4,500,1024]{2,1,0:T(8,128)(2,1)} %reshape.160), kind=kOutput, calls=%fused_computation.53 | convolution fusion | flops 4204539904 | bytes 18497152 | tf_op jit(solution)/shard_map/dot_general | solution.py:55
  473.1 5.7 %all_to_all.42 = bf16[2000,2,512]{2,1,0:T(2,128)(2,1)} reshape(bf16[4,500,1024]{2,1,0:T(8,128)(2,1)} %add_convert_fusion) | data formatting | bytes 8192000 | tf_op jit(solution)/shard_map/all_to_all | solution.py:114
  481.6 8.0 %all_to_all.51 = bf16[2000,2,512]{2,0,1:T(8,128)(2,1)} all-to-all(bf16[2000,2,512]{2,0,1:T(8,128)(2,1)S(1)} %copy.28), channel_id=1, replica_groups=mesh['leaf'=16,'head'=2] {'head'}, dimensions={1} | all-to-all | bytes 8192000 | tf_op jit(solution)/shard_map/all_to_all | solution.py:114
  489.6 5.1 %reshape.163 = bf16[8,500,512]{2,1,0:T(8,128)(2,1)} reshape(bf16[2,2000,512]{2,1,0:T(8,128)(2,1)} %bitcast.56) | data formatting | bytes 8192000 | tf_op jit(solution)/shard_map/reshape | solution.py:115
  494.7 5.5 %copy.29 = bf16[8,500,512]{2,0,1:T(8,128)(2,1)} copy(bf16[8,500,512]{2,1,0:T(8,128)(2,1)} %reshape.163) | data formatting | bytes 8192000 | tf_op jit(solution)/shard_map/reshape | solution.py:115
  (69 shorter events, 51.2 us)
Async XLA Ops:
  6.5 36.4 %copy-start = (bf16[2048,512]{1,0:T(8,128)(2,1)S(1)}, bf16[2048,512]{1,0:T(8,128)(2,1)}, u32[]{:S(2)}) copy-start(bf16[2048,512]{1,0:T(8,128)(2,1)} %param.14) | copy-start | bytes 6291460
  83.1 8.4 %copy-start.2 = (bf16[1024,512]{1,0:T(8,128)(2,1)S(1)}, bf16[1024,512]{1,0:T(8,128)(2,1)}, u32[]{:S(2)}) copy-start(bf16[1024,512]{1,0:T(8,128)(2,1)} %param.18) | copy-start | bytes 3145732
  83.1 9.8 %copy-start.3 = (bf16[1024,512]{1,0:T(8,128)(2,1)S(1)}, bf16[1024,512]{1,0:T(8,128)(2,1)}, u32[]{:S(2)}) copy-start(bf16[1024,512]{1,0:T(8,128)(2,1)} %param.16) | copy-start | bytes 3145732
  83.1 191.6 %all-to-all-start.1 = ((bf16[16,500,512]{2,1,0:T(8,128)(2,1)}), bf16[16,500,512]{2,1,0:T(8,128)(2,1)}, u32[]{:S(2)}, u32[]{:S(2)}) async-start(bf16[16,500,512]{2,1,0:T(8,128)(2,1)} %broadcast_select_fusion), calls=%async_computation.1 | async-start | bytes 16515072 | tf_op jit(solution)/shard_map/all_to_all | solution.py:82
  91.4 2.9 copy-start.4
  91.4 22.6 %all-gather.11.cloned.1.call-start = ((), (), s32[]{:S(2)}) async-start(), calls=%async_computation.6 | async-start | bytes 3145728 | tf_op jit(solution)/shard_map/all_gather | solution.py:92
  92.8 3.6 copy-start.5
  92.8 28.3 %all-gather.7.cloned.1.call-start = ((), (), s32[]{:S(2)}) async-start(), calls=%async_computation.4 | async-start | bytes 3145728 | tf_op jit(solution)/shard_map/all_gather | solution.py:90
  94.2 40.2 %all-gather.9.cloned.1.call-start = ((), (), s32[]{:S(2)}) async-start(), calls=%async_computation.5 | async-start | bytes 3145728 | tf_op jit(solution)/shard_map/all_gather | solution.py:91
  95.6 364.8 %all-gather.13.cloned.1.call-start = ((), (), s32[]{:S(2)}) async-start(), calls=%async_computation.7 | async-start | bytes 3145728 | tf_op jit(solution)/shard_map/all_gather | solution.py:93
  100.6 7.3 %copy-start.8 = (f32[512]{0:T(512)S(1)}, f32[512]{0:T(512)}, u32[]{:S(2)}) copy-start(f32[512]{0:T(512)} %param.20) | copy-start | bytes 6148
  100.6 11.4 %copy-start.9 = (f32[512]{0:T(512)S(1)}, f32[512]{0:T(512)}, u32[]{:S(2)}) copy-start(f32[512]{0:T(512)} %param.21) | copy-start | bytes 6148
  460.4 9.9 %copy-start.6 = (f32[2,1,512]{2,1,0:T(1,128)S(1)}, f32[2,1,512]{2,1,0:T(1,128)}, u32[]{:S(2)}) copy-start(f32[2,1,512]{2,1,0:T(1,128)} %all-gather) | copy-start | bytes 12292
  460.4 9.9 %copy-start.7 = (f32[2,1,512]{2,1,0:T(1,128)S(1)}, f32[2,1,512]{2,1,0:T(1,128)}, u32[]{:S(2)}) copy-start(f32[2,1,512]{2,1,0:T(1,128)} %all-gather.1) | copy-start | bytes 12292
  489.6 10.6 %copy-start.1 = (bf16[2048,512]{1,0:T(8,128)(2,1)S(1)}, bf16[2048,512]{1,0:T(8,128)(2,1)}, u32[]{:S(2)}) copy-start(bf16[2048,512]{1,0:T(8,128)(2,1)} %param.14) | copy-start | bytes 6291460
Sparse Core Ops, SparseCore 0:
  93.8 13.9 all-gather.10
  109.3 11.7 all-gather.6
  122.6 11.7 all-gather.8
  135.8 11.7 all-gather.12
where the time goes:
time: 508 us; the launch traced here: 507 us
  local copies, waits for them, and re-layouts  169 us (33%)
  waiting for transfers between devices  154 us (30%)
  matrix products  104 us (20%)
  blocking collectives  32.6 us (6%)
  other arithmetic  25.1 us (5%)
  between operations  13.4 us (3%)
  starting transfers between devices  8.48 us (2%)
    all_to_all x1, waiting for transfers between devices, shards(): lax.all_to_all(found, 'leaf', split_axis=0, concat_axis=0, tiled=True)  133 us
    sub x4, matrix products, one_user(): weights = jax.nn.softmax(scores, axis=-1).astype(jnp.bfloat16)  39.8 us
    dot_general x4, matrix products, one_user(): lax.dot_general(values, weights, (((2,), (2,)), ((0,), (0,))), preferred_...  35.1 us
    gather x2, local copies, waits for them, and re-layouts, shards(): jnp.take(table, lax.all_to_all(requests, 'leaf', split_axis=0, concat_axi...  32.8 us
    gather x1, local copies, waits for them, and re-layouts, shards(): jnp.take(fetched.reshape(n_leaf * capacity, cols), target, axis=0)  21.8 us
    scatter x1, local copies, waits for them, and re-layouts, shards(): requests = jnp.zeros((n_leaf * capacity,), jnp.int32).at[target].set(loca...  19.3 us
    dot_general x1, matrix products, project_heads(): lax.dot_general(weight_rows, rows3, (((0,), (2,)), ((), ())), preferred_e...  19.3 us
    all_to_all x1, local copies, waits for them, and re-layouts, shards(): lax.all_to_all(x, 'head', split_axis=0, concat_axis=1, tiled=True)  18.6 us
  transfers between devices with their start and end apart: 5, of which 3 were waited for; matrix products, arithmetic and copies ran while one was open for 39% of the time, Pallas kernels for 0%

commit v1 on v0

v1 whole, which is shorter than its diff:
```python
import functools
import math

import jax
import jax.numpy as jnp
from jax import lax
from jax.experimental import pallas as pl
from jax.experimental.pallas import tpu as pltpu
from jax.sharding import PartitionSpec as P

HEAD_DIM = 64
PAIR = 2 * HEAD_DIM
SPLIT = 2


def mm(a, b):
    return jnp.dot(a, b, preferred_element_type=jnp.float32)


def attend_kernel(length, xo_ref, xt_ref, qo, qt, ko, kt, vo, vt, ctx_ref):
    xo, xt = xo_ref[0], xt_ref[0]
    padded, cols = xo.shape
    scale = math.log2(math.e) / HEAD_DIM**0.5
    q = ((mm(xo, qo[...]) + mm(xt, qt[...])) * scale).astype(jnp.bfloat16)
    k = (mm(xo, ko[...]) + mm(xt, kt[...])).astype(jnp.bfloat16)
    v = (mm(xo, vo[...]) + mm(xt, vt[...])).astype(jnp.bfloat16)
    low = lax.broadcasted_iota(jnp.int32, (padded, PAIR), 1) < HEAD_DIM
    real = lax.broadcasted_iota(jnp.int32, (padded, PAIR), 0) < length
    ones = jnp.where(real, 1.0, 0.0).astype(jnp.bfloat16)
    for pair in range(cols // PAIR):
        lanes = slice(pair * PAIR, (pair + 1) * PAIR)
        qp, kp, vp = q[:, lanes], k[:, lanes], v[:, lanes]
        vx = jnp.concatenate([jnp.where(real, vp, jnp.zeros_like(vp)), ones], axis=1)
        halves = []
        for mask in (low, jnp.logical_not(low)):
            qm = jnp.where(mask, qp, jnp.zeros_like(qp))
            s = lax.dot_general(
                qm, kp, (((1,), (1,)), ((), ())), preferred_element_type=jnp.float32
            )
            e = jnp.exp2(s - jnp.max(s, axis=1, keepdims=True)).astype(jnp.bfloat16)
            o = mm(e, vx)
            halves.append(o[:, :PAIR] / o[:, PAIR:])
        ctx_ref[0, :, lanes] = jnp.where(low, halves[0], halves[1]).astype(jnp.bfloat16)


def attend(length, xo, xt, weights):
    users, padded, cols = xo.shape
    block = pl.BlockSpec((1, padded, cols), lambda u: (u, 0, 0))
    whole = pl.BlockSpec((cols, cols), lambda u: (0, 0))
    flops = users * (12 * padded * cols * cols + 8 * padded * padded * cols)
    return pl.pallas_call(
        functools.partial(attend_kernel, length),
        grid=(users,),
        out_shape=jax.ShapeDtypeStruct(xo.shape, jnp.bfloat16),
        in_specs=[block, block] + [whole] * 6,
        out_specs=block,
        compiler_params=pltpu.CompilerParams(vmem_limit_bytes=44 * 1024 * 1024),
        cost_estimate=pl.CostEstimate(
            flops=flops,
            bytes_accessed=3 * xo.size * 2 + 12 * cols * cols,
            transcendentals=users * (cols // HEAD_DIM) * padded * padded,
        ),
        name="attend",
    )(xo, xt, *weights)


def finish_kernel(length, xo_ref, xt_ref, co_ref, ct_ref, oo, to, ot, tt, gain, bias, out_ref):
    co, ct = co_ref[0], ct_ref[0]
    yo = xo_ref[0].astype(jnp.float32) + mm(co, oo[...]) + mm(ct, to[...])
    yt = xt_ref[0].astype(jnp.float32) + mm(co, ot[...]) + mm(ct, tt[...])
    width = 2 * yo.shape[1]
    mean = jnp.sum(yo + yt, axis=1, keepdims=True) / width
    var = jnp.sum(yo * yo + yt * yt, axis=1, keepdims=True) / width - mean * mean
    normed = (yo - mean) * lax.rsqrt(var + 1e-05) * gain[...] + bias[...]
    out_ref[0] = normed[:length].astype(jnp.bfloat16)


def finish(length, xo, xt, co, ct, weights, gain, bias):
    users, padded, cols = xo.shape
    block = pl.BlockSpec((1, padded, cols), lambda u: (u, 0, 0))
    whole = pl.BlockSpec((cols, cols), lambda u: (0, 0))
    row = pl.BlockSpec((1, cols), lambda u: (0, 0))
    return pl.pallas_call(
        functools.partial(finish_kernel, length),
        grid=(users,),
        out_shape=jax.ShapeDtypeStruct((users, length, cols), jnp.bfloat16),
        in_specs=[block] * 4 + [whole] * 4 + [row] * 2,
        out_specs=pl.BlockSpec((1, length, cols), lambda u: (u, 0, 0)),
        compiler_params=pltpu.CompilerParams(vmem_limit_bytes=44 * 1024 * 1024),
        cost_estimate=pl.CostEstimate(
            flops=users * 8 * padded * cols * cols,
            bytes_accessed=5 * xo.size * 2 + 8 * cols * cols,
            transcendentals=0,
        ),
        name="finish",
    )(xo, xt, co, ct, *weights, gain, bias)


def swap(a):
    return lax.ppermute(a, "head", [(0, 1), (1, 0)])


def build_requests(owner, local_row, n_leaf, capacity):
    onehot = owner[None, :] == jnp.arange(n_leaf, dtype=jnp.int32)[:, None]
    counted = onehot.astype(jnp.int32)
    rank = jnp.sum((jnp.cumsum(counted, axis=1) - counted) * counted, axis=0)
    high, low = local_row // 64, local_row % 64
    parts = jnp.concatenate(
        [jnp.where(onehot, high[None, :], 0), jnp.where(onehot, low[None, :], 0)], axis=0
    ).astype(jnp.bfloat16)
    slots = (rank[:, None] == jnp.arange(capacity, dtype=jnp.int32)[None, :]).astype(jnp.bfloat16)
    placed = mm(parts, slots).astype(jnp.int32)
    return placed[:n_leaf] * 64 + placed[n_leaf:], owner * capacity + rank


def shards(cand_owner, cand_row, table, position, w_query, w_key, w_value, w_out, gain, shift_bias):
    users, length, _ = cand_owner.shape
    total = users * length
    cols = table.shape[1]
    n_leaf = lax.axis_size("leaf")
    head = lax.axis_index("head")
    own, other = head * cols, (1 - head) * cols
    capacity = (max(2, 2 * total // n_leaf) + 7) // 8 * 8
    padded = (length + 15) // 16 * 16

    requests, target = build_requests(
        cand_owner.reshape(total), cand_row.reshape(total), n_leaf, capacity
    )
    asked = lax.all_to_all(requests, "leaf", split_axis=0, concat_axis=0, tiled=True)
    found = table.at[asked.reshape(n_leaf * capacity)].get(mode="promise_in_bounds")
    fetched = lax.all_to_all(
        found.reshape(n_leaf, capacity, cols), "leaf", split_axis=0, concat_axis=0, tiled=True
    ).reshape(n_leaf * capacity, cols)

    def rows_of(w, start):
        return lax.dynamic_slice(w, (start, 0), (cols, cols))

    def columns_of(w, start):
        return lax.dynamic_slice(w, (0, start), (cols, cols))

    qkv = [rows_of(w, start) for w in (w_query, w_key, w_value) for start in (own, other)]
    w_out_other = swap(w_out)
    mix = [columns_of(w, start) for start in (own, other) for w in (w_out, w_out_other)]

    target = jnp.pad(target.reshape(users, length), ((0, 0), (0, padded - length)), mode="edge")
    shift = jnp.pad(position, ((0, padded - length), (0, 0)), mode="edge").astype(jnp.float32)
    part = users // SPLIT
    mine, theirs, context, context_other = [], [], [], []
    for index in range(SPLIT):
        places = target[index * part : (index + 1) * part].reshape(part * padded)
        rows = fetched.at[places].get(mode="promise_in_bounds").reshape(part, padded, cols)
        x = (rows.astype(jnp.float32) + shift[None]).astype(jnp.bfloat16)
        mine.append(x)
        theirs.append(swap(x))
    for index in range(SPLIT):
        c = attend(length, mine[index], theirs[index], qkv)
        context.append(c)
        context_other.append(swap(c))
    done = [
        finish(
            length,
            mine[index],
            theirs[index],
            context[index],
            context_other[index],
            mix,
            gain.reshape(1, cols),
            shift_bias.reshape(1, cols),
        )
        for index in range(SPLIT)
    ]
    return jnp.concatenate(done, axis=0)


def solution(mesh):
    return jax.shard_map(
        shards,
        mesh=mesh,
        in_specs=(
            P("leaf", None, None),
            P("leaf", None),
            P("leaf", "head"),
            P(None, "head"),
            P(None, "head"),
            P(None, "head"),
            P(None, "head"),
            P("head", None),
            P("head"),
            P("head"),
        ),
        out_specs=P("leaf", None, "head"),
        check_vma=False,
    )
```

time: 508 us -> 341 us (0.67)
  local copies, waits for them, and re-layouts: 169 us -> 61 us
  matrix products: 104 us -> 1.47 us
  Pallas kernels: 0 us -> 55.1 us
  waiting for transfers between devices: 154 us -> 188 us
  blocking collectives: 32.6 us -> 8.89 us
  between operations: 13.4 us -> 0.37 us
  other arithmetic: 25.1 us -> 13.1 us
    dot_general x6 -> x1, matrix products: 64.2 us -> 1.47 us  [mm(): return jnp.dot(a, b, preferred_element_type=jnp.float32)]
    pallas_call x0 -> x4, Pallas kernels: none -> 55.1 us  [the longest x2 38.8 us: attend(): pl.pallas_call(functools.partial(attend_kernel, length), grid=(users,), o...]
    all_to_all x1, waiting for transfers between devices: 133 us -> 181 us  [shards(): lax.all_to_all(found.reshape(n_leaf, capacity, cols), 'leaf', split_axis=...]
    sub x4 -> x0, matrix products: 39.8 us -> none  [one_user(): weights = jax.nn.softmax(scores, axis=-1).astype(jnp.bfloat16)]
    reshape x7 -> x4, local copies, waits for them, and re-layouts: 32.3 us -> 0.28 us  [the longest x1 0.12 us: shards(): asked.reshape(n_leaf * capacity)]
    all_to_all x3 -> x0, local copies, waits for them, and re-layouts: 27.1 us -> none  [the longest x1 18.6 us: shards(): lax.all_to_all(x, 'head', split_axis=0, concat_axis=1, tiled=True)]
    all_gather x4 -> x0, waiting for transfers between devices: 20.4 us -> none  [the longest x1 13.3 us: shards(): lax.all_gather(w_key, 'head', axis=1, tiled=True)]
    scatter x1 -> x0, local copies, waits for them, and re-layouts: 19.3 us -> none  [shards(): requests = jnp.zeros((n_leaf * capacity,), jnp.int32).at[target].set(loca...]
  transfers between devices with their start and end apart: 5 -> 6, of which waited for: 3 -> 3; matrix products, arithmetic and copies ran while one was open for 39% -> 1% of each run, Pallas kernels for 0% -> 14%
where the time goes in v1:
time: 341 us; the launch traced here: 340 us
  waiting for transfers between devices  188 us (55%)
  local copies, waits for them, and re-layouts  61 us (18%)
  Pallas kernels  55.1 us (16%)
  other arithmetic  13.1 us (4%)
  starting transfers between devices  12.2 us (4%)
  blocking collectives  8.89 us (3%)
    all_to_all x1, waiting for transfers between devices, shards(): lax.all_to_all(found.reshape(n_leaf, capacity, cols), 'leaf', split_axis=...  181 us
    pallas_call x2, Pallas kernels, attend(): pl.pallas_call(functools.partial(attend_kernel, length), grid=(users,), o...  38.8 us
    gather x2, local copies, waits for them, and re-layouts, shards(): fetched.at[places].get(mode='promise_in_bounds').reshape(part, padded, cols)  27.4 us
    gather x1, local copies, waits for them, and re-layouts, shards(): table.at[asked.reshape(n_leaf * capacity)].get(mode='promise_in_bounds')  23.6 us
    pallas_call x2, Pallas kernels, finish(): pl.pallas_call(functools.partial(finish_kernel, length), grid=(users,), o...  16.3 us
    all_to_all x1, blocking collectives, shards(): lax.all_to_all(requests, 'leaf', split_axis=0, concat_axis=0, tiled=True)  8.89 us
    all_to_all x1, starting transfers between devices, shards(): lax.all_to_all(found.reshape(n_leaf, capacity, cols), 'leaf', split_axis=...  8.18 us
    ppermute x5, waiting for transfers between devices, swap(): return lax.ppermute(a, 'head', [(0, 1), (1, 0)])  7.45 us
  transfers between devices with their start and end apart: 6, of which 3 were waited for; matrix products, arithmetic and copies ran while one was open for 1% of the time, Pallas kernels for 14%

profile of v1, /device:TPU:29, one launch (start us, length us, event | category | flops | bytes accessed | tf_op | source)
XLA Modules:
  0.0 340.4 jit_solution(13469130600070002003)
XLA Ops:
  0.0 0.9 broadcast_multiply_fusion
  1.1 4.6 %reduce-window.6 = s32[16,32,128]{2,1,0:T(8,128)S(1)} reduce-window(s32[16,32,128]{2,1,0:T(8,128)S(1)} %bitcast.39, s32[]{:T(128)} %constant.40.clone.1), window={size=1x1x128 pad=0_0x0_0x127_0}, to_apply=%region_0.0 | reduce-window | flops 8323072 | bytes 524292 | tf_op jit(solution)/shard_map/reduce-window
  5.8 0.5 slice_reduce_fusion
  6.2 0.2 reduce-window.9
  6.6 0.2 copy.22
  7.0 1.5 fusion.4
  8.5 8.9 %all_to_all.14 = s32[16,1,504]{2,1,0:T(1,128)S(1)} all-to-all(s32[16,1,504]{2,1,0:T(1,128)S(1)} %copy.13), channel_id=1, replica_groups=mesh['leaf'=16,'head'=2] {'leaf'}, dimensions={0} | all-to-all | bytes 64512 | tf_op jit(solution)/shard_map/all_to_all | solution.py:129
  17.7 23.6 %gather_fusion = bf16[8064,512]{1,0:T(8,128)(2,1)} fusion(bf16[2048,512]{1,0:T(8,128)(2,1)S(1)} %copy-done, s32[8192]{0:T(1024)S(1)} %pad_clamp_fusion), kind=kCustom, calls=%fused_computation | custom fusion | bytes 16547328 | tf_op jit(solution)/shard_map/gather | solution.py:130
  41.4 8.2 %all-to-all-start.1 = ((bf16[16,504,512]{2,1,0:T(8,128)(2,1)}), bf16[16,504,512]{2,1,0:T(8,128)(2,1)}, u32[]{:S(2)}, u32[]{:S(2)}) async-start(bf16[16,504,512]{2,1,0:T(8,128)(2,1)} %bitcast.36), calls=%async_computation.1 | async-start | bytes 16515072 | tf_op jit(solution)/shard_map/all_to_all | solution.py:131
  49.6 0.2 slice_reduce_fusion.1
  50.0 0.7 slice_reduce_fusion.2
  50.7 1.2 maximum_convert_fusion
  52.0 180.8 %all-to-all-done.1 = bf16[16,504,512]{2,1,0:T(8,128)(2,1)} async-done(((bf16[16,504,512]{2,1,0:T(8,128)(2,1)}), bf16[16,504,512]{2,1,0:T(8,128)(2,1)}, u32[]{:S(2)}, u32[]{:S(2)}) %all-to-all-start.1) | async-done | bytes 8257568 | tf_op jit(solution)/shard_map/all_to_all | solution.py:131
  232.8 13.7 %gather_fusion.2 = bf16[2048,512]{1,0:T(8,128)(2,1)} fusion(bf16[8064,512]{1,0:T(8,128)(2,1)} %bitcast.2, s32[2048]{0:T(1024)S(1)} %broadcast_clamp_fusion), kind=kCustom, calls=%fused_computation.2 | custom fusion | bytes 4202496 | tf_op jit(solution)/shard_map/gather | solution.py:151
  246.5 13.7 %gather_fusion.1 = bf16[2048,512]{1,0:T(8,128)(2,1)} fusion(bf16[8064,512]{1,0:T(8,128)(2,1)} %bitcast.2, s32[2048]{0:T(1024)S(1)} %broadcast_clamp_fusion.1), kind=kCustom, calls=%fused_computation.1 | custom fusion | bytes 4202496 | tf_op jit(solution)/shard_map/gather | solution.py:151
  260.2 5.2 %fusion.2 = (bf16[4,512,512]{2,1,0:T(8,128)(2,1)}, bf16[4,512,512]{2,1,0:T(8,128)(2,1)}) fusion(bf16[4,512,512]{2,1,0:T(8,128)(2,1)} %bitcast.38, f32[512,512]{1,0:T(8,128)S(1)} %maximum_convert_fusion, bf16[4,512,512]{2,1,0:T(8,128)(2,1)} %bitcast.37), kind=kLoop, calls=%fused_computation.8 | loop fusion | flops 6291456 | bytes 9437184 | tf_op jit(solution)/shard_map/convert_element_type | solution.py:152
  265.4 3.0 collective-permute-start
  268.4 1.4 constant_dynamic-slice_fusion.8
  269.8 0.2 copy-done.6
  269.9 0.2 constant_dynamic-slice_fusion.4
  270.1 2.4 collective-permute-done.xt_ref
  272.5 19.1 %attend.2.co_ref = bf16[4,512,512]{2,1,0:T(8,128)(2,1)S(1)} custom-call(bf16[4,512,512]{2,1,0:T(8,128)(2,1)} %get-tuple-element.5.xo_ref, bf16[4,512,512]{2,1,0:T(8,128)(2,1)} %collective-permute-done.xt_ref, bf16[512,512]{1,0:T(8,128)(2,1)S(1)} %get-tuple-element.16.qo, bf16[512,512]{1,0:T(8,128)(2,1)S(1)} %get-tuple-element.15.qt, ...), custom_call_target="tpu_custom_call" | custom-call | flops 10737418240 | bytes 9437184 | tf_op jit(solution)/shard_map/attend/pallas_call | solution.py:51
  291.6 0.4 collective-permute-start.1
  292.1 19.7 %attend.3.co_ref = bf16[4,512,512]{2,1,0:T(8,128)(2,1)S(1)} custom-call(bf16[4,512,512]{2,1,0:T(8,128)(2,1)} %get-tuple-element.6.xo_ref, bf16[4,512,512]{2,1,0:T(8,128)(2,1)} %collective-permute-done.3.xt_ref, bf16[512,512]{1,0:T(8,128)(2,1)S(1)} %get-tuple-element.16.qo, bf16[512,512]{1,0:T(8,128)(2,1)S(1)} %get-tuple-element.15.qt, ...), custom_call_target="tpu_custom_call" | custom-call | flops 10737418240 | bytes 9437184 | tf_op jit(solution)/shard_map/attend/pallas_call | solution.py:51
  311.8 0.4 collective-permute-start.4
  312.5 5.0 %collective-permute-done.2 = bf16[512,1024]{1,0:T(8,128)(2,1)S(1)} collective-permute-done((bf16[512,1024]{1,0:T(8,128)(2,1)S(1)}, bf16[512,1024]{1,0:T(8,128)(2,1)S(1)}, u32[]{:S(2)}, u32[]{:S(2)}) %collective-permute-start.2) | collective-permute-done | bytes 1048608 | tf_op jit(solution)/shard_map/ppermute | solution.py:100
  317.7 1.3 copy-done.9
  319.0 8.1 %finish.2 = bf16[4,500,512]{2,1,0:T(8,128)(2,1)S(1)} custom-call(bf16[4,512,512]{2,1,0:T(8,128)(2,1)} %get-tuple-element.5.xo_ref, bf16[4,512,512]{2,1,0:T(8,128)(2,1)} %collective-permute-done.xt_ref, bf16[4,512,512]{2,1,0:T(8,128)(2,1)} %copy-done.1, bf16[4,512,512]{2,1,0:T(8,128)(2,1)} %copy-done.9, bf16[512,512]{1,0:T(8,128)(2,1)S(1)} %get-tuple-element.10.oo, ...), custom_call_target="tpu_custom_call" | custom-call | flops 4294967296 | bytes 12582912 | tf_op jit(solution)/shard_map/finish/pallas_call | solution.py:83
  327.2 1.3 copy-done.10
  328.5 8.1 %finish.3 = bf16[4,500,512]{2,1,0:T(8,128)(2,1)S(1)} custom-call(bf16[4,512,512]{2,1,0:T(8,128)(2,1)} %get-tuple-element.6.xo_ref, bf16[4,512,512]{2,1,0:T(8,128)(2,1)} %collective-permute-done.3.xt_ref, bf16[4,512,512]{2,1,0:T(8,128)(2,1)} %copy-done.2, bf16[4,512,512]{2,1,0:T(8,128)(2,1)} %copy-done.10, bf16[512,512]{1,0:T(8,128)(2,1)S(1)} %get-tuple-element.10.oo, ...), custom_call_target="tpu_custom_call" | custom-call | flops 4294967296 | bytes 12582912 | tf_op jit(solution)/shard_map/finish/pallas_call | solution.py:83
  336.7 0.4 pad_maximum_fusion
  337.0 3.4 copy.14
  (51 shorter events, 1.6 us)
Async XLA Ops:
  0.0 17.7 %copy-start = (bf16[2048,512]{1,0:T(8,128)(2,1)S(1)}, bf16[2048,512]{1,0:T(8,128)(2,1)}, u32[]{:S(2)}) copy-start(bf16[2048,512]{1,0:T(8,128)(2,1)} %param.12) | copy-start | bytes 6291460
  0.0 6.7 %copy-start.8 = (s32[8,500]{1,0:T(8,128)S(1)}, s32[8,500]{1,0:T(8,128)}, u32[]{:S(2)}) copy-start(s32[8,500]{1,0:T(8,128)} %param.11) | copy-start | bytes 48004
  41.4 191.5 %all-to-all-start.1 = ((bf16[16,504,512]{2,1,0:T(8,128)(2,1)}), bf16[16,504,512]{2,1,0:T(8,128)(2,1)}, u32[]{:S(2)}, u32[]{:S(2)}) async-start(bf16[16,504,512]{2,1,0:T(8,128)(2,1)} %bitcast.36), calls=%async_computation.1 | async-start | bytes 16515072 | tf_op jit(solution)/shard_map/all_to_all | solution.py:131
  265.4 4.4 %copy-start.5 = (bf16[1024,512]{1,0:T(8,128)(2,1)S(1)}, bf16[1024,512]{1,0:T(8,128)(2,1)}, u32[]{:S(2)}) copy-start(bf16[1024,512]{1,0:T(8,128)(2,1)} %param.16) | copy-start | bytes 3145732
  265.4 7.2 %collective-permute-start = (bf16[4,512,512]{2,1,0:T(8,128)(2,1)}, bf16[4,512,512]{2,1,0:T(8,128)(2,1)}, u32[]{:S(2)}, u32[]{:S(2)}) collective-permute-start(bf16[4,512,512]{2,1,0:T(8,128)(2,1)} %get-tuple-element.5.xo_ref), channel_id=1, source_target_pairs={{0,1},{1,0},{2,3},{3,2},{4,5},{5,4},{6,7},{7,6},{8,9},{9,8},{10,11... | collective-permute-start | bytes 6291464 | tf_op jit(solution)/shard_map/ppermute | solution.py:100
  268.4 23.7 %collective-permute-start.3 = (bf16[4,512,512]{2,1,0:T(8,128)(2,1)}, bf16[4,512,512]{2,1,0:T(8,128)(2,1)}, u32[]{:S(2)}, u32[]{:S(2)}) collective-permute-start(bf16[4,512,512]{2,1,0:T(8,128)(2,1)} %get-tuple-element.6.xo_ref), channel_id=1, source_target_pairs={{0,1},{1,0},{2,3},{3,2},{4,5},{5,4},{6,7},{7,6},{8,9},{9,8},{10,11... | collective-permute-start | bytes 6291464 | tf_op jit(solution)/shard_map/ppermute | solution.py:100
  268.4 1.5 copy-start.6
  291.6 20.2 %copy-start.1 = (bf16[4,512,512]{2,1,0:T(8,128)(2,1)}, bf16[4,512,512]{2,1,0:T(8,128)(2,1)S(1)}, u32[]{:S(2)}) copy-start(bf16[4,512,512]{2,1,0:T(8,128)(2,1)S(1)} %attend.2.co_ref) | copy-start | bytes 6291460
  291.6 20.7 %copy-start.7 = (bf16[512,1024]{1,0:T(8,128)(2,1)S(1)}, bf16[512,1024]{1,0:T(8,128)(2,1)}, u32[]{:S(2)}) copy-start(bf16[512,1024]{1,0:T(8,128)(2,1)} %param.17) | copy-start | bytes 3145732
  291.6 26.1 %collective-permute-start.1 = (bf16[4,512,512]{2,1,0:T(8,128)(2,1)S(1)}, bf16[4,512,512]{2,1,0:T(8,128)(2,1)S(1)}, u32[]{:S(2)}, u32[]{:S(2)}) collective-permute-start(bf16[4,512,512]{2,1,0:T(8,128)(2,1)S(1)} %attend.2.co_ref), channel_id=1, source_target_pairs={{0,1},{1,0},{2,3},{3,2},{4,5},{5,4},{6,7},{7,6},{8,9},{9,8},{10,11... | collective-permute-start | bytes 6291464 | tf_op jit(solution)/shard_map/ppermute | solution.py:100
  311.8 5.9 %copy-start.2 = (bf16[4,512,512]{2,1,0:T(8,128)(2,1)}, bf16[4,512,512]{2,1,0:T(8,128)(2,1)S(1)}, u32[]{:S(2)}) copy-start(bf16[4,512,512]{2,1,0:T(8,128)(2,1)S(1)} %attend.3.co_ref) | copy-start | bytes 6291460
  311.8 7.2 %copy-start.3 = (f32[512]{0:T(512)S(1)}, f32[512]{0:T(512)}, u32[]{:S(2)}) copy-start(f32[512]{0:T(512)} %param.18) | copy-start | bytes 6148
  311.8 7.2 %copy-start.4 = (f32[512]{0:T(512)S(1)}, f32[512]{0:T(512)}, u32[]{:S(2)}) copy-start(f32[512]{0:T(512)} %param.19) | copy-start | bytes 6148
  311.8 15.3 %collective-permute-start.4 = (bf16[4,512,512]{2,1,0:T(8,128)(2,1)S(1)}, bf16[4,512,512]{2,1,0:T(8,128)(2,1)S(1)}, u32[]{:S(2)}, u32[]{:S(2)}) collective-permute-start(bf16[4,512,512]{2,1,0:T(8,128)(2,1)S(1)} %attend.3.co_ref), channel_id=1, source_target_pairs={{0,1},{1,0},{2,3},{3,2},{4,5},{5,4},{6,7},{7,6},{8,9},{9,8},{10,11... | collective-permute-start | bytes 6291464 | tf_op jit(solution)/shard_map/ppermute | solution.py:100
  312.3 5.3 %collective-permute-start.2 = (bf16[512,1024]{1,0:T(8,128)(2,1)S(1)}, bf16[512,1024]{1,0:T(8,128)(2,1)S(1)}, u32[]{:S(2)}, u32[]{:S(2)}) collective-permute-start(bf16[512,1024]{1,0:T(8,128)(2,1)S(1)} %copy-done.7), channel_id=1, source_target_pairs={{0,1},{1,0},{2,3},{3,2},{4,5},{5,4},{6,7},{7,6},{8,9},{9,8},{10,11... | collective-permute-start | bytes 3145736 | tf_op jit(solution)/shard_map/ppermute | solution.py:100
  317.7 1.3 copy-start.9
  327.2 1.3 copy-start.10

commit v2 on v1

--- a/solution.py
+++ b/solution.py
@@ -11,6 +11,7 @@
 HEAD_DIM = 64
 PAIR = 2 * HEAD_DIM
 SPLIT = 2
+CUTS = (0, 3, 9, 14)
 
 
 def mm(a, b):
@@ -100,17 +101,21 @@
     return lax.ppermute(a, "head", [(0, 1), (1, 0)])
 
 
-def build_requests(owner, local_row, n_leaf, capacity):
+def rank_candidates(owner, n_leaf):
     onehot = owner[None, :] == jnp.arange(n_leaf, dtype=jnp.int32)[:, None]
     counted = onehot.astype(jnp.int32)
-    rank = jnp.sum((jnp.cumsum(counted, axis=1) - counted) * counted, axis=0)
+    return onehot, jnp.sum((jnp.cumsum(counted, axis=1) - counted) * counted, axis=0)
+
+
+def place_requests(onehot, rank, local_row, capacity):
+    n_leaf = onehot.shape[0]
     high, low = local_row // 64, local_row % 64
     parts = jnp.concatenate(
         [jnp.where(onehot, high[None, :], 0), jnp.where(onehot, low[None, :], 0)], axis=0
     ).astype(jnp.bfloat16)
     slots = (rank[:, None] == jnp.arange(capacity, dtype=jnp.int32)[None, :]).astype(jnp.bfloat16)
     placed = mm(parts, slots).astype(jnp.int32)
-    return placed[:n_leaf] * 64 + placed[n_leaf:], owner * capacity + rank
+    return placed[:n_leaf] * 64 + placed[n_leaf:]
 
 
 def shards(cand_owner, cand_row, table, position, w_query, w_key, w_value, w_out, gain, shift_bias):
@@ -123,14 +128,41 @@
     capacity = (max(2, 2 * total // n_leaf) + 7) // 8 * 8
     padded = (length + 15) // 16 * 16
 
-    requests, target = build_requests(
-        cand_owner.reshape(total), cand_row.reshape(total), n_leaf, capacity
-    )
-    asked = lax.all_to_all(requests, "leaf", split_axis=0, concat_axis=0, tiled=True)
-    found = table.at[asked.reshape(n_leaf * capacity)].get(mode="promise_in_bounds")
-    fetched = lax.all_to_all(
-        found.reshape(n_leaf, capacity, cols), "leaf", split_axis=0, concat_axis=0, tiled=True
-    ).reshape(n_leaf * capacity, cols)
+    half = n_leaf // 2
+    groups = [list(range(half)), list(range(half, n_leaf))]
+    side = lax.axis_index("leaf") // half
+    mirror = [(i, (i + half) % n_leaf) for i in range(n_leaf)]
+    cuts = [table.shape[0] * c // 32 for c in CUTS]
+
+    def exchange(a):
+        return lax.all_to_all(
+            a, "leaf", split_axis=0, concat_axis=0, tiled=True, axis_index_groups=groups
+        )
+
+    def mirrored(piece, beside):
+        moved = lax.ppermute(table[cuts[piece] : cuts[piece + 1]], "leaf", mirror)
+        return lax.optimization_barrier((moved, beside))
+
+    owner = cand_owner.reshape(total)
+    onehot, rank = rank_candidates(owner, n_leaf)
+    far_a, rank = mirrored(0, rank)
+    requests = place_requests(onehot, rank, cand_row.reshape(total), capacity)
+    sides = requests.reshape(2, half, capacity)
+    near = lax.dynamic_index_in_dim(sides, side, 0, keepdims=False)
+    far = lax.dynamic_index_in_dim(sides, 1 - side, 0, keepdims=False)
+    far_b, asked = mirrored(1, exchange(jnp.concatenate([near, far], axis=1)))
+
+    def find(block, places):
+        return block.at[places.reshape(half * capacity)].get(mode="promise_in_bounds")
+
+    def send(found):
+        return exchange(found.reshape(half, capacity, cols)).reshape(half * capacity, cols)
+
+    far_c, found = mirrored(2, find(table, asked[:, :capacity]))
+    fetched_near = send(found)
+    far_d = lax.ppermute(table[cuts[3] :], "leaf", mirror)
+    far_table = jnp.concatenate([far_a, far_b, far_c, far_d], axis=0)
+    fetched_far = send(find(far_table, asked[:, capacity:]))
 
     def rows_of(w, start):
         return lax.dynamic_slice(w, (start, 0), (cols, cols))
@@ -139,16 +171,25 @@
         return lax.dynamic_slice(w, (0, start), (cols, cols))
 
     qkv = [rows_of(w, start) for w in (w_query, w_key, w_value) for start in (own, other)]
-    w_out_other = swap(w_out)
+    fetched_near, w_out_other = lax.optimization_barrier((fetched_near, swap(w_out)))
     mix = [columns_of(w, start) for start in (own, other) for w in (w_out, w_out_other)]
 
+    target = owner * capacity + rank
+    is_near = target // (half * capacity) == side
+    target = target % (half * capacity)
+    is_near = jnp.pad(is_near.reshape(users, length), ((0, 0), (0, padded - length)), mode="edge")
     target = jnp.pad(target.reshape(users, length), ((0, 0), (0, padded - length)), mode="edge")
     shift = jnp.pad(position, ((0, padded - length), (0, 0)), mode="edge").astype(jnp.float32)
     part = users // SPLIT
     mine, theirs, context, context_other = [], [], [], []
     for index in range(SPLIT):
-        places = target[index * part : (index + 1) * part].reshape(part * padded)
-        rows = fetched.at[places].get(mode="promise_in_bounds").reshape(part, padded, cols)
+        some = slice(index * part, (index + 1) * part)
+        places = target[some].reshape(part * padded)
+        rows_near, rows_far = (
+            f.at[places].get(mode="promise_in_bounds").reshape(part, padded, cols)
+            for f in (fetched_near, fetched_far)
+        )
+        rows = jnp.where(is_near[some][:, :, None], rows_near, rows_far)
         x = (rows.astype(jnp.float32) + shift[None]).astype(jnp.bfloat16)
         mine.append(x)
         theirs.append(swap(x))

time: 341 us -> 307 us (0.900); the launches traced: 340 us -> 302 us
  waiting for transfers between devices: 188 us -> 103 us
  local copies, waits for them, and re-layouts: 61 us -> 98.9 us
  starting transfers between devices: 12.2 us -> 28.9 us
  blocking collectives: 8.89 us -> 0 us
    all_to_all x1 -> x3, waiting for transfers between devices: 181 us -> 20.8 us  [exchange(): lax.all_to_all(a, 'leaf', split_axis=0, concat_axis=0, tiled=True, axis_i...]
    ppermute x0 -> x4, waiting for transfers between devices: none -> 77.7 us  [the longest x1 67.5 us: shards(): far_d = lax.ppermute(table[cuts[3]:], 'leaf', mirror)]
    gather x3 -> x6, local copies, waits for them, and re-layouts: 51 us -> 82.7 us  [the longest x4 48.1 us: shards(): f.at[places].get(mode='promise_in_bounds').reshape(part, padded, cols)]
    all_to_all x1 -> x3, starting transfers between devices: 8.18 us -> 21.4 us  [exchange(): lax.all_to_all(a, 'leaf', split_axis=0, concat_axis=0, tiled=True, axis_i...]
    all_to_all x1 -> x0, blocking collectives: 8.89 us -> none  [shards(): lax.all_to_all(requests, 'leaf', split_axis=0, concat_axis=0, tiled=True)]
    slice x0 -> x6, local copies, waits for them, and re-layouts: none -> 3.76 us  [the longest x3 3.43 us: mirrored(): moved = lax.ppermute(table[cuts[piece]:cuts[piece + 1]], 'leaf', mirror)]
  transfers between devices with their start and end apart: 6 -> 12, of which waited for: 3 -> 5; matrix products, arithmetic and copies ran while one was open for 1% -> 25% of each run, Pallas kernels for 14% -> 15%
where the time goes in v2:
time: 307 us; the launch traced here: 302 us
  waiting for transfers between devices  103 us (34%)
  local copies, waits for them, and re-layouts  98.9 us (32%)
  Pallas kernels  54.7 us (18%)
  starting transfers between devices  28.9 us (9%)
  other arithmetic  14.5 us (5%)
    ppermute x1, waiting for transfers between devices, shards(): far_d = lax.ppermute(table[cuts[3]:], 'leaf', mirror)  67.5 us
    gather x4, local copies, waits for them, and re-layouts, shards(): f.at[places].get(mode='promise_in_bounds').reshape(part, padded, cols)  48.1 us
    pallas_call x2, Pallas kernels, attend(): pl.pallas_call(functools.partial(attend_kernel, length), grid=(users,), o...  38.6 us
    gather x2, local copies, waits for them, and re-layouts, find(): block.at[places.reshape(half * capacity)].get(mode='promise_in_bounds')  34.6 us
    all_to_all x3, starting transfers between devices, exchange(): lax.all_to_all(a, 'leaf', split_axis=0, concat_axis=0, tiled=True, axis_i...  21.4 us
    all_to_all x3, waiting for transfers between devices, exchange(): lax.all_to_all(a, 'leaf', split_axis=0, concat_axis=0, tiled=True, axis_i...  20.8 us
    pallas_call x2, Pallas kernels, finish(): pl.pallas_call(functools.partial(finish_kernel, length), grid=(users,), o...  16.1 us
    ppermute x3, waiting for transfers between devices, mirrored(): moved = lax.ppermute(table[cuts[piece]:cuts[piece + 1]], 'leaf', mirror)  10.2 us
  transfers between devices with their start and end apart: 12, of which 5 were waited for; matrix products, arithmetic and copies ran while one was open for 25% of the time, Pallas kernels for 15%

profile of v2, /device:TPU:29, one launch (start us, length us, event | category | flops | bytes accessed | tf_op | source)
XLA Modules:
  0.0 301.9 jit_solution(6167563024699063475)
XLA Ops:
  0.0 1.6 slice.63
  1.7 1.0 slice.71
  2.7 2.4 collective-permute-start.2
  6.0 4.6 %reduce-window.6 = s32[16,32,128]{2,1,0:T(8,128)S(1)} reduce-window(s32[16,32,128]{2,1,0:T(8,128)S(1)} %bitcast.51, s32[]{:T(128)} %constant.72.clone.1), window={size=1x1x128 pad=0_0x0_0x127_0}, to_apply=%region_0.1 | reduce-window | flops 8323072 | bytes 524292 | tf_op jit(solution)/shard_map/reduce-window
  11.9 10.2 %collective-permute-done = bf16[192,512]{1,0:T(8,128)(2,1)S(1)} collective-permute-done((bf16[192,512]{1,0:T(8,128)(2,1)}, bf16[192,512]{1,0:T(8,128)(2,1)S(1)}, u32[]{:S(2)}, u32[]{:S(2)}) %collective-permute-start) | collective-permute-done | bytes 196640 | tf_op jit(solution)/shard_map/ppermute | solution.py:143
  22.1 1.5 fusion.2
  24.3 4.6 %all-to-all-start = ((s32[8,1,1008]{2,1,0:T(1,128)}), s32[8,1,1008]{2,1,0:T(1,128)S(1)}, u32[]{:S(2)}, u32[]{:S(2)}) async-start(s32[8,1,1008]{2,1,0:T(1,128)} %all_to_all.14), calls=%async_computation | async-start | bytes 65536 | tf_op jit(solution)/shard_map/all_to_all | solution.py:138
  29.7 1.8 all-to-all-done
  31.7 17.3 %gather_fusion = bf16[4032,512]{1,0:T(8,128)(2,1)} fusion(bf16[2048,512]{1,0:T(8,128)(2,1)S(1)} %copy-done.4, s32[4096]{0:T(1024)S(1)} %pad_clamp_fusion.1), kind=kCustom, calls=%fused_computation | custom fusion | bytes 8273664 | tf_op jit(solution)/shard_map/gather | solution.py:156
  49.0 6.4 %all-to-all-start.1 = ((bf16[8,504,512]{2,1,0:T(8,128)(2,1)}), bf16[8,504,512]{2,1,0:T(8,128)(2,1)}, u32[]{:S(2)}, u32[]{:S(2)}) async-start(bf16[8,504,512]{2,1,0:T(8,128)(2,1)} %bitcast.46), calls=%async_computation.1 | async-start | bytes 8257536 | tf_op jit(solution)/shard_map/all_to_all | solution.py:138
  55.7 67.5 %collective-permute-done.4 = bf16[1152,512]{1,0:T(8,128)(2,1)} collective-permute-done((bf16[1152,512]{1,0:T(8,128)(2,1)S(1)}, bf16[1152,512]{1,0:T(8,128)(2,1)}, u32[]{:S(2)}, u32[]{:S(2)}) %collective-permute-start.4) | collective-permute-done | bytes 1179680 | tf_op jit(solution)/shard_map/ppermute | solution.py:163
  123.2 1.6 pad_maximum_fusion.1
  124.8 17.3 %gather_fusion.2 = bf16[4032,512]{1,0:T(8,128)(2,1)} fusion(bf16[2048,512]{1,0:T(8,128)(2,1)S(1)} %pad_maximum_fusion.1, s32[4096]{0:T(1024)S(1)} %pad_clamp_fusion), kind=kCustom, calls=%fused_computation.2 | custom fusion | bytes 8273664 | tf_op jit(solution)/shard_map/gather | solution.py:156
  142.1 10.4 %all-to-all-start.2 = ((bf16[8,504,512]{2,1,0:T(8,128)(2,1)}), bf16[8,504,512]{2,1,0:T(8,128)(2,1)}, u32[]{:S(2)}, u32[]{:S(2)}) async-start(bf16[8,504,512]{2,1,0:T(8,128)(2,1)} %bitcast.45), calls=%async_computation.2 | async-start | bytes 8257536 | tf_op jit(solution)/shard_map/all_to_all | solution.py:138
  152.6 3.5 %collective-permute-start.3 = (bf16[512,1024]{1,0:T(8,128)(2,1)S(1)}, bf16[512,1024]{1,0:T(8,128)(2,1)S(1)}, u32[]{:S(2)}, u32[]{:S(2)}) collective-permute-start(bf16[512,1024]{1,0:T(8,128)(2,1)S(1)} %copy-done.7), channel_id=1, source_target_pairs={{0,1},{1,0},{2,3},{3,2},{4,5},{5,4},{6,7},{7,6},{8,9},{9,8},{10,11... | collective-permute-start | bytes 3145736 | tf_op jit(solution)/shard_map/ppermute | solution.py:101
  156.8 1.2 maximum_convert_fusion
  159.0 12.3 %gather_fusion.4 = bf16[2048,512]{1,0:T(8,128)(2,1)} fusion(bf16[4032,512]{1,0:T(8,128)(2,1)} %bitcast.5, s32[2048]{0:T(1024)S(1)} %broadcast_clamp_fusion), kind=kCustom, calls=%fused_computation.4 | custom fusion | bytes 4202496 | tf_op jit(solution)/shard_map/gather | solution.py:189
  171.3 12.0 %gather_fusion.1 = bf16[2048,512]{1,0:T(8,128)(2,1)} fusion(bf16[4032,512]{1,0:T(8,128)(2,1)} %bitcast.5, s32[2048]{0:T(1024)S(1)} %broadcast_clamp_fusion.1), kind=kCustom, calls=%fused_computation.1 | custom fusion | bytes 4202496 | tf_op jit(solution)/shard_map/gather | solution.py:189
  183.2 19.0 %all-to-all-done.2 = bf16[8,504,512]{2,1,0:T(8,128)(2,1)} async-done(((bf16[8,504,512]{2,1,0:T(8,128)(2,1)}), bf16[8,504,512]{2,1,0:T(8,128)(2,1)}, u32[]{:S(2)}, u32[]{:S(2)}) %all-to-all-start.2) | async-done | bytes 4128800 | tf_op jit(solution)/shard_map/all_to_all | solution.py:138
  202.2 11.9 %gather_fusion.5 = bf16[2048,512]{1,0:T(8,128)(2,1)} fusion(bf16[4032,512]{1,0:T(8,128)(2,1)} %bitcast.10, s32[2048]{0:T(1024)S(1)} %broadcast_clamp_fusion), kind=kCustom, calls=%fused_computation.5 | custom fusion | bytes 4202496 | tf_op jit(solution)/shard_map/gather | solution.py:189
  214.2 11.9 %gather_fusion.3 = bf16[2048,512]{1,0:T(8,128)(2,1)} fusion(bf16[4032,512]{1,0:T(8,128)(2,1)} %bitcast.10, s32[2048]{0:T(1024)S(1)} %broadcast_clamp_fusion.1), kind=kCustom, calls=%fused_computation.3 | custom fusion | bytes 4202496 | tf_op jit(solution)/shard_map/gather | solution.py:189
  226.1 5.1 %add_convert_fusion.1 = (bf16[4,512,512]{2,1,0:T(8,128)(2,1)}, bf16[4,512,512]{2,1,0:T(8,128)(2,1)S(1)}) fusion(f32[512,512]{1,0:T(8,128)S(1)} %maximum_convert_fusion, bf16[4,512,512]{2,1,0:T(8,128)(2,1)} %bitcast.48, bf16[4,512,512]{2,1,0:T(8,128)(2,1)} %bitcast.50, pred[4,512]{1,0:T(4,128)(4,1)S(1)} %get-tuple-element.44, ...), kind=kLoop, calls=%fused_computation.9 | loop fusion | flops 8388608 | bytes 13635584 | tf_op jit(solution)/shard_map/convert_element_type | solution.py:193
  231.8 1.4 constant_dynamic-slice_fusion.8
  233.6 4.5 %collective-permute-done.5.xt_ref = bf16[4,512,512]{2,1,0:T(8,128)(2,1)} collective-permute-done((bf16[4,512,512]{2,1,0:T(8,128)(2,1)}, bf16[4,512,512]{2,1,0:T(8,128)(2,1)}, u32[]{:S(2)}, u32[]{:S(2)}) %collective-permute-start.5) | collective-permute-done | bytes 2097184 | tf_op jit(solution)/shard_map/ppermute | solution.py:101
  238.1 19.1 %attend.2.co_ref = bf16[4,512,512]{2,1,0:T(8,128)(2,1)S(1)} custom-call(bf16[4,512,512]{2,1,0:T(8,128)(2,1)} %get-tuple-element.21.xo_ref, bf16[4,512,512]{2,1,0:T(8,128)(2,1)} %collective-permute-done.5.xt_ref, bf16[512,512]{1,0:T(8,128)(2,1)S(1)} %get-tuple-element.32.qo, bf16[512,512]{1,0:T(8,128)(2,1)S(1)} %get-tuple-element.31.qt, ...), custom_call_target="tpu_custom_call" | custom-call | flops 10737418240 | bytes 9437184 | tf_op jit(solution)/shard_map/attend/pallas_call | solution.py:52
  257.7 19.5 %attend.3.co_ref = bf16[4,512,512]{2,1,0:T(8,128)(2,1)S(1)} custom-call(bf16[4,512,512]{2,1,0:T(8,128)(2,1)S(1)} %get-tuple-element.22.xo_ref, bf16[4,512,512]{2,1,0:T(8,128)(2,1)} %collective-permute-done.7.xt_ref, bf16[512,512]{1,0:T(8,128)(2,1)S(1)} %get-tuple-element.32.qo, bf16[512,512]{1,0:T(8,128)(2,1)S(1)} %get-tuple-element.31.qt, ...), custom_call_target="tpu_custom_call" | custom-call | flops 10737418240 | bytes 9437184 | tf_op jit(solution)/shard_map/attend/pallas_call | solution.py:52
  277.8 1.4 copy-done.10
  279.4 1.4 copy-done.13
  280.7 8.1 %finish.2 = bf16[4,500,512]{2,1,0:T(8,128)(2,1)S(1)} custom-call(bf16[4,512,512]{2,1,0:T(8,128)(2,1)} %get-tuple-element.21.xo_ref, bf16[4,512,512]{2,1,0:T(8,128)(2,1)} %collective-permute-done.5.xt_ref, bf16[4,512,512]{2,1,0:T(8,128)(2,1)} %copy-done, bf16[4,512,512]{2,1,0:T(8,128)(2,1)} %copy-done.13, bf16[512,512]{1,0:T(8,128)(2,1)S(1)} %get-tuple-element.26.oo, ...), custom_call_target="tpu_custom_call" | custom-call | flops 4294967296 | bytes 12582912 | tf_op jit(solution)/shard_map/finish/pallas_call | solution.py:84
  288.9 1.3 copy-done.14
  290.2 8.0 %finish.3 = bf16[4,500,512]{2,1,0:T(8,128)(2,1)S(1)} custom-call(bf16[4,512,512]{2,1,0:T(8,128)(2,1)S(1)} %get-tuple-element.22.xo_ref, bf16[4,512,512]{2,1,0:T(8,128)(2,1)} %collective-permute-done.7.xt_ref, bf16[4,512,512]{2,1,0:T(8,128)(2,1)} %copy-done.1, bf16[4,512,512]{2,1,0:T(8,128)(2,1)} %copy-done.14, bf16[512,512]{1,0:T(8,128)(2,1)S(1)} %get-tuple-element.26.oo, ...), custom_call_target="tpu_custom_call" | custom-call | flops 4294967296 | bytes 12582912 | tf_op jit(solution)/shard_map/finish/pallas_call | solution.py:84
  298.6 3.4 %copy.16 = bf16[8,500,512]{2,0,1:T(8,128)(2,1)} copy(bf16[8,500,512]{2,1,0:T(8,128)(2,1)S(1)} %pad_maximum_fusion) | data formatting | bytes 8192000 | tf_op jit(solution)/shard_map/concatenate | solution.py:213
  (89 shorter events, 8.3 us)
Async XLA Ops:
  1.6 10.0 %copy-start.12 = (s32[8,500]{1,0:T(8,128)S(1)}, s32[8,500]{1,0:T(8,128)}, u32[]{:S(2)}) copy-start(s32[8,500]{1,0:T(8,128)} %param.11) | copy-start | bytes 48004
  1.6 20.5 %collective-permute-start = (bf16[192,512]{1,0:T(8,128)(2,1)}, bf16[192,512]{1,0:T(8,128)(2,1)S(1)}, u32[]{:S(2)}, u32[]{:S(2)}) collective-permute-start(bf16[192,512]{1,0:T(8,128)(2,1)} %slice.63), channel_id=1, source_target_pairs={{0,16},{2,18},{4,20},{6,22},{8,24},{10,26},{12,28},{14,30},{16,0},... | collective-permute-start | bytes 589832 | tf_op jit(solution)/shard_map/ppermute | solution.py:143
  2.7 28.8 %collective-permute-start.2 = (bf16[384,512]{1,0:T(8,128)(2,1)S(1)}, bf16[384,512]{1,0:T(8,128)(2,1)S(1)}, u32[]{:S(2)}, u32[]{:S(2)}) collective-permute-start(bf16[384,512]{1,0:T(8,128)(2,1)S(1)} %slice.71), channel_id=1, source_target_pairs={{0,16},{2,18},{4,20},{6,22},{8,24},{10,26},{12,28},{14,30},{16,0},... | collective-permute-start | bytes 1179656 | tf_op jit(solution)/shard_map/ppermute | solution.py:143
  11.6 17.2 %copy-start.4 = (bf16[2048,512]{1,0:T(8,128)(2,1)S(1)}, bf16[2048,512]{1,0:T(8,128)(2,1)}, u32[]{:S(2)}) copy-start(bf16[2048,512]{1,0:T(8,128)(2,1)} %param.12) | copy-start | bytes 6291460
  24.3 7.2 %all-to-all-start = ((s32[8,1,1008]{2,1,0:T(1,128)}), s32[8,1,1008]{2,1,0:T(1,128)S(1)}, u32[]{:S(2)}, u32[]{:S(2)}) async-start(s32[8,1,1008]{2,1,0:T(1,128)} %all_to_all.14), calls=%async_computation | async-start | bytes 65536 | tf_op jit(solution)/shard_map/all_to_all | solution.py:138
  29.7 19.3 %collective-permute-start.1 = (bf16[320,512]{1,0:T(8,128)(2,1)}, bf16[320,512]{1,0:T(8,128)(2,1)}, u32[]{:S(2)}, u32[]{:S(2)}) collective-permute-start(bf16[320,512]{1,0:T(8,128)(2,1)} %slice.70), channel_id=1, source_target_pairs={{0,16},{2,18},{4,20},{6,22},{8,24},{10,26},{12,28},{14,30},{16,0},... | collective-permute-start | bytes 983048 | tf_op jit(solution)/shard_map/ppermute | solution.py:143
  31.5 17.5 %copy-start.11 = (bf16[384,512]{1,0:T(8,128)(2,1)}, bf16[384,512]{1,0:T(8,128)(2,1)S(1)}, u32[]{:S(2)}) copy-start(bf16[384,512]{1,0:T(8,128)(2,1)S(1)} %collective-permute-done.2) | copy-start | bytes 1179652
  49.0 93.1 %all-to-all-start.1 = ((bf16[8,504,512]{2,1,0:T(8,128)(2,1)}), bf16[8,504,512]{2,1,0:T(8,128)(2,1)}, u32[]{:S(2)}, u32[]{:S(2)}) async-start(bf16[8,504,512]{2,1,0:T(8,128)(2,1)} %bitcast.46), calls=%async_computation.1 | async-start | bytes 8257536 | tf_op jit(solution)/shard_map/all_to_all | solution.py:138
  55.5 67.7 %collective-permute-start.4 = (bf16[1152,512]{1,0:T(8,128)(2,1)S(1)}, bf16[1152,512]{1,0:T(8,128)(2,1)}, u32[]{:S(2)}, u32[]{:S(2)}) collective-permute-start(bf16[1152,512]{1,0:T(8,128)(2,1)S(1)} %slice.78), channel_id=1, source_target_pairs={{0,16},{2,18},{4,20},{6,22},{8,24},{10,26},{12,28},{14,30},{16,0},... | collective-permute-start | bytes 3538952 | tf_op jit(solution)/shard_map/ppermute | solution.py:163
  142.1 10.4 %copy-start.7 = (bf16[512,1024]{1,0:T(8,128)(2,1)S(1)}, bf16[512,1024]{1,0:T(8,128)(2,1)}, u32[]{:S(2)}) copy-start(bf16[512,1024]{1,0:T(8,128)(2,1)} %param.17) | copy-start | bytes 3145732
  142.1 60.1 %all-to-all-start.2 = ((bf16[8,504,512]{2,1,0:T(8,128)(2,1)}), bf16[8,504,512]{2,1,0:T(8,128)(2,1)}, u32[]{:S(2)}, u32[]{:S(2)}) async-start(bf16[8,504,512]{2,1,0:T(8,128)(2,1)} %bitcast.45), calls=%async_computation.2 | async-start | bytes 8257536 | tf_op jit(solution)/shard_map/all_to_all | solution.py:138
  152.6 6.4 %collective-permute-start.3 = (bf16[512,1024]{1,0:T(8,128)(2,1)S(1)}, bf16[512,1024]{1,0:T(8,128)(2,1)S(1)}, u32[]{:S(2)}, u32[]{:S(2)}) collective-permute-start(bf16[512,1024]{1,0:T(8,128)(2,1)S(1)} %copy-done.7), channel_id=1, source_target_pairs={{0,1},{1,0},{2,3},{3,2},{4,5},{5,4},{6,7},{7,6},{8,9},{9,8},{10,11... | collective-permute-start | bytes 3145736 | tf_op jit(solution)/shard_map/ppermute | solution.py:101
  159.0 12.3 %copy-start.9 = (bf16[512,1024]{1,0:T(8,128)(2,1)}, bf16[512,1024]{1,0:T(8,128)(2,1)S(1)}, u32[]{:S(2)}) copy-start(bf16[512,1024]{1,0:T(8,128)(2,1)S(1)} %collective-permute-done.3) | copy-start | bytes 3145732
  231.2 1.9 copy-start.5
  231.2 6.9 %collective-permute-start.5 = (bf16[4,512,512]{2,1,0:T(8,128)(2,1)}, bf16[4,512,512]{2,1,0:T(8,128)(2,1)}, u32[]{:S(2)}, u32[]{:S(2)}) collective-permute-start(bf16[4,512,512]{2,1,0:T(8,128)(2,1)} %get-tuple-element.21.xo_ref), channel_id=1, source_target_pairs={{0,1},{1,0},{2,3},{3,2},{4,5},{5,4},{6,7},{7,6},{8,9},{9,8},{10,11... | collective-permute-start | bytes 6291464 | tf_op jit(solution)/shard_map/ppermute | solution.py:101
  231.7 26.0 %collective-permute-start.7 = (bf16[4,512,512]{2,1,0:T(8,128)(2,1)S(1)}, bf16[4,512,512]{2,1,0:T(8,128)(2,1)}, u32[]{:S(2)}, u32[]{:S(2)}) collective-permute-start(bf16[4,512,512]{2,1,0:T(8,128)(2,1)S(1)} %get-tuple-element.22.xo_ref), channel_id=1, source_target_pairs={{0,1},{1,0},{2,3},{3,2},{4,5},{5,4},{6,7},{7,6},{8,9},{9,8},{10,11... | collective-permute-start | bytes 6291464 | tf_op jit(solution)/shard_map/ppermute | solution.py:101
  231.8 1.6 copy-start.6
  257.2 20.0 %copy-start = (bf16[4,512,512]{2,1,0:T(8,128)(2,1)}, bf16[4,512,512]{2,1,0:T(8,128)(2,1)S(1)}, u32[]{:S(2)}) copy-start(bf16[4,512,512]{2,1,0:T(8,128)(2,1)S(1)} %attend.2.co_ref) | copy-start | bytes 6291460
  257.2 20.5 %copy-start.8 = (bf16[512,1024]{1,0:T(8,128)(2,1)S(1)}, bf16[512,1024]{1,0:T(8,128)(2,1)}, u32[]{:S(2)}) copy-start(bf16[512,1024]{1,0:T(8,128)(2,1)} %param.17) | copy-start | bytes 3145732
  257.2 22.1 %collective-permute-start.6 = (bf16[4,512,512]{2,1,0:T(8,128)(2,1)S(1)}, bf16[4,512,512]{2,1,0:T(8,128)(2,1)S(1)}, u32[]{:S(2)}, u32[]{:S(2)}) collective-permute-start(bf16[4,512,512]{2,1,0:T(8,128)(2,1)S(1)} %attend.2.co_ref), channel_id=1, source_target_pairs={{0,1},{1,0},{2,3},{3,2},{4,5},{5,4},{6,7},{7,6},{8,9},{9,8},{10,11... | collective-permute-start | bytes 6291464 | tf_op jit(solution)/shard_map/ppermute | solution.py:101
  277.2 2.1 copy-start.1
  277.2 2.0 copy-start.10
  277.2 3.5 %copy-start.2 = (f32[512]{0:T(512)S(1)}, f32[512]{0:T(512)}, u32[]{:S(2)}) copy-start(f32[512]{0:T(512)} %param.18) | copy-start | bytes 6148
  277.3 3.5 %copy-start.3 = (f32[512]{0:T(512)S(1)}, f32[512]{0:T(512)}, u32[]{:S(2)}) copy-start(f32[512]{0:T(512)} %param.19) | copy-start | bytes 6148
  277.3 11.6 %collective-permute-start.8 = (bf16[4,512,512]{2,1,0:T(8,128)(2,1)S(1)}, bf16[4,512,512]{2,1,0:T(8,128)(2,1)S(1)}, u32[]{:S(2)}, u32[]{:S(2)}) collective-permute-start(bf16[4,512,512]{2,1,0:T(8,128)(2,1)S(1)} %attend.3.co_ref), channel_id=1, source_target_pairs={{0,1},{1,0},{2,3},{3,2},{4,5},{5,4},{6,7},{7,6},{8,9},{9,8},{10,11... | collective-permute-start | bytes 6291464 | tf_op jit(solution)/shard_map/ppermute | solution.py:101
  279.3 1.4 copy-start.13
  288.9 1.3 copy-start.14

commit v3 on v2

--- a/solution.py
+++ b/solution.py
@@ -11,7 +11,7 @@
 HEAD_DIM = 64
 PAIR = 2 * HEAD_DIM
 SPLIT = 2
-CUTS = (0, 3, 9, 14)
+CUTS = (0, 1, 11, 19)
 
 
 def mm(a, b):

time: 307 us -> 316 us (1.029)
  waiting for transfers between devices: 103 us -> 112 us
    ppermute x3, waiting for transfers between devices: 10.2 us -> 23.6 us  [mirrored(): moved = lax.ppermute(table[cuts[piece]:cuts[piece + 1]], 'leaf', mirror)]
    ppermute x1, waiting for transfers between devices: 67.5 us -> 60.1 us  [shards(): far_d = lax.ppermute(table[cuts[3]:], 'leaf', mirror)]
  transfers between devices with their start and end apart: 12 -> 12, of which waited for: 5 -> 6; matrix products, arithmetic and copies ran while one was open for 25% -> 25% of each run, Pallas kernels for 15% -> 15%
where the time goes in v3:
time: 316 us; the launch traced here: 309 us
  waiting for transfers between devices  112 us (35%)
  local copies, waits for them, and re-layouts  98.9 us (31%)
  Pallas kernels  54.7 us (17%)
  starting transfers between devices  27.4 us (9%)
  other arithmetic  14.3 us (5%)
    ppermute x1, waiting for transfers between devices, shards(): far_d = lax.ppermute(table[cuts[3]:], 'leaf', mirror)  60.1 us
    gather x4, local copies, waits for them, and re-layouts, shards(): f.at[places].get(mode='promise_in_bounds').reshape(part, padded, cols)  48.1 us
    pallas_call x2, Pallas kernels, attend(): pl.pallas_call(functools.partial(attend_kernel, length), grid=(users,), o...  38.6 us
    gather x2, local copies, waits for them, and re-layouts, find(): block.at[places.reshape(half * capacity)].get(mode='promise_in_bounds')  34.5 us
    all_to_all x3, waiting for transfers between devices, exchange(): lax.all_to_all(a, 'leaf', split_axis=0, concat_axis=0, tiled=True, axis_i...  23.9 us
    ppermute x3, waiting for transfers between devices, mirrored(): moved = lax.ppermute(table[cuts[piece]:cuts[piece + 1]], 'leaf', mirror)  23.6 us
    all_to_all x3, starting transfers between devices, exchange(): lax.all_to_all(a, 'leaf', split_axis=0, concat_axis=0, tiled=True, axis_i...  20.3 us
    pallas_call x2, Pallas kernels, finish(): pl.pallas_call(functools.partial(finish_kernel, length), grid=(users,), o...  16.1 us
  transfers between devices with their start and end apart: 12, of which 6 were waited for; matrix products, arithmetic and copies ran while one was open for 25% of the time, Pallas kernels for 15%

profile of v3, /device:TPU:29, one launch (start us, length us, event | category | flops | bytes accessed | tf_op | source)
XLA Modules:
  0.0 309.5 jit_solution(13794828141330551602)
XLA Ops:
  0.9 1.1 slice.71
  2.0 2.4 collective-permute-start.2
  5.4 4.6 %reduce-window.6 = s32[16,32,128]{2,1,0:T(8,128)S(1)} reduce-window(s32[16,32,128]{2,1,0:T(8,128)S(1)} %bitcast.51, s32[]{:T(128)} %constant.72.clone.1), window={size=1x1x128 pad=0_0x0_0x127_0}, to_apply=%region_0.1 | reduce-window | flops 8323072 | bytes 524292 | tf_op jit(solution)/shard_map/reduce-window
  11.2 9.5 %collective-permute-done = bf16[64,512]{1,0:T(8,128)(2,1)S(1)} collective-permute-done((bf16[64,512]{1,0:T(8,128)(2,1)S(1)}, bf16[64,512]{1,0:T(8,128)(2,1)S(1)}, u32[]{:S(2)}, u32[]{:S(2)}) %collective-permute-start) | collective-permute-done | bytes 65568 | tf_op jit(solution)/shard_map/ppermute | solution.py:143
  20.7 1.5 fusion.2
  23.0 4.6 %all-to-all-start = ((s32[8,1,1008]{2,1,0:T(1,128)}), s32[8,1,1008]{2,1,0:T(1,128)S(1)}, u32[]{:S(2)}, u32[]{:S(2)}) async-start(s32[8,1,1008]{2,1,0:T(1,128)} %all_to_all.14), calls=%async_computation | async-start | bytes 65536 | tf_op jit(solution)/shard_map/all_to_all | solution.py:138
  27.7 4.4 %all-to-all-done = s32[8,1,1008]{2,1,0:T(1,128)S(1)} async-done(((s32[8,1,1008]{2,1,0:T(1,128)}), s32[8,1,1008]{2,1,0:T(1,128)S(1)}, u32[]{:S(2)}, u32[]{:S(2)}) %all-to-all-start) | async-done | bytes 32288 | tf_op jit(solution)/shard_map/all_to_all | solution.py:138
  32.1 14.1 %collective-permute-done.2 = bf16[640,512]{1,0:T(8,128)(2,1)} collective-permute-done((bf16[640,512]{1,0:T(8,128)(2,1)S(1)}, bf16[640,512]{1,0:T(8,128)(2,1)}, u32[]{:S(2)}, u32[]{:S(2)}) %collective-permute-start.2) | collective-permute-done | bytes 655392 | tf_op jit(solution)/shard_map/ppermute | solution.py:143
  47.0 17.3 %gather_fusion = bf16[4032,512]{1,0:T(8,128)(2,1)} fusion(bf16[2048,512]{1,0:T(8,128)(2,1)S(1)} %copy-done.4, s32[4096]{0:T(1024)S(1)} %pad_clamp_fusion.1), kind=kCustom, calls=%fused_computation | custom fusion | bytes 8273664 | tf_op jit(solution)/shard_map/gather | solution.py:156
  64.3 4.7 %all-to-all-start.1 = ((bf16[8,504,512]{2,1,0:T(8,128)(2,1)}), bf16[8,504,512]{2,1,0:T(8,128)(2,1)}, u32[]{:S(2)}, u32[]{:S(2)}) async-start(bf16[8,504,512]{2,1,0:T(8,128)(2,1)} %bitcast.46), calls=%async_computation.1 | async-start | bytes 8257536 | tf_op jit(solution)/shard_map/all_to_all | solution.py:138
  70.3 60.1 %collective-permute-done.4 = bf16[832,512]{1,0:T(8,128)(2,1)S(1)} collective-permute-done((bf16[832,512]{1,0:T(8,128)(2,1)}, bf16[832,512]{1,0:T(8,128)(2,1)S(1)}, u32[]{:S(2)}, u32[]{:S(2)}) %collective-permute-start.4) | collective-permute-done | bytes 852000 | tf_op jit(solution)/shard_map/ppermute | solution.py:163
  130.4 1.4 pad_maximum_fusion.1
  131.8 17.3 %gather_fusion.2 = bf16[4032,512]{1,0:T(8,128)(2,1)} fusion(bf16[2048,512]{1,0:T(8,128)(2,1)S(1)} %pad_maximum_fusion.1, s32[4096]{0:T(1024)S(1)} %pad_clamp_fusion), kind=kCustom, calls=%fused_computation.2 | custom fusion | bytes 8273664 | tf_op jit(solution)/shard_map/gather | solution.py:156
  149.1 11.0 %all-to-all-start.2 = ((bf16[8,504,512]{2,1,0:T(8,128)(2,1)}), bf16[8,504,512]{2,1,0:T(8,128)(2,1)}, u32[]{:S(2)}, u32[]{:S(2)}) async-start(bf16[8,504,512]{2,1,0:T(8,128)(2,1)} %bitcast.45), calls=%async_computation.2 | async-start | bytes 8257536 | tf_op jit(solution)/shard_map/all_to_all | solution.py:138
  160.1 3.0 collective-permute-start.3
  163.8 1.2 maximum_convert_fusion
  166.0 12.3 %gather_fusion.4 = bf16[2048,512]{1,0:T(8,128)(2,1)} fusion(bf16[4032,512]{1,0:T(8,128)(2,1)} %bitcast.5, s32[2048]{0:T(1024)S(1)} %broadcast_clamp_fusion), kind=kCustom, calls=%fused_computation.4 | custom fusion | bytes 4202496 | tf_op jit(solution)/shard_map/gather | solution.py:189
  178.3 12.0 %gather_fusion.1 = bf16[2048,512]{1,0:T(8,128)(2,1)} fusion(bf16[4032,512]{1,0:T(8,128)(2,1)} %bitcast.5, s32[2048]{0:T(1024)S(1)} %broadcast_clamp_fusion.1), kind=kCustom, calls=%fused_computation.1 | custom fusion | bytes 4202496 | tf_op jit(solution)/shard_map/gather | solution.py:189
  190.2 19.5 %all-to-all-done.2 = bf16[8,504,512]{2,1,0:T(8,128)(2,1)} async-done(((bf16[8,504,512]{2,1,0:T(8,128)(2,1)}), bf16[8,504,512]{2,1,0:T(8,128)(2,1)}, u32[]{:S(2)}, u32[]{:S(2)}) %all-to-all-start.2) | async-done | bytes 4128800 | tf_op jit(solution)/shard_map/all_to_all | solution.py:138
  209.7 11.9 %gather_fusion.5 = bf16[2048,512]{1,0:T(8,128)(2,1)} fusion(bf16[4032,512]{1,0:T(8,128)(2,1)} %bitcast.10, s32[2048]{0:T(1024)S(1)} %broadcast_clamp_fusion), kind=kCustom, calls=%fused_computation.5 | custom fusion | bytes 4202496 | tf_op jit(solution)/shard_map/gather | solution.py:189
  221.7 11.9 %gather_fusion.3 = bf16[2048,512]{1,0:T(8,128)(2,1)} fusion(bf16[4032,512]{1,0:T(8,128)(2,1)} %bitcast.10, s32[2048]{0:T(1024)S(1)} %broadcast_clamp_fusion.1), kind=kCustom, calls=%fused_computation.3 | custom fusion | bytes 4202496 | tf_op jit(solution)/shard_map/gather | solution.py:189
  233.6 5.1 %add_convert_fusion.1 = (bf16[4,512,512]{2,1,0:T(8,128)(2,1)}, bf16[4,512,512]{2,1,0:T(8,128)(2,1)S(1)}) fusion(f32[512,512]{1,0:T(8,128)S(1)} %maximum_convert_fusion, bf16[4,512,512]{2,1,0:T(8,128)(2,1)} %bitcast.48, bf16[4,512,512]{2,1,0:T(8,128)(2,1)} %bitcast.50, pred[4,512]{1,0:T(4,128)(4,1)S(1)} %get-tuple-element.44, ...), kind=kLoop, calls=%fused_computation.9 | loop fusion | flops 8388608 | bytes 13635584 | tf_op jit(solution)/shard_map/convert_element_type | solution.py:193
  239.3 1.4 constant_dynamic-slice_fusion.8
  241.1 4.5 %collective-permute-done.5.xt_ref = bf16[4,512,512]{2,1,0:T(8,128)(2,1)} collective-permute-done((bf16[4,512,512]{2,1,0:T(8,128)(2,1)}, bf16[4,512,512]{2,1,0:T(8,128)(2,1)}, u32[]{:S(2)}, u32[]{:S(2)}) %collective-permute-start.5) | collective-permute-done | bytes 2097184 | tf_op jit(solution)/shard_map/ppermute | solution.py:101
  245.6 19.1 %attend.2.co_ref = bf16[4,512,512]{2,1,0:T(8,128)(2,1)S(1)} custom-call(bf16[4,512,512]{2,1,0:T(8,128)(2,1)} %get-tuple-element.21.xo_ref, bf16[4,512,512]{2,1,0:T(8,128)(2,1)} %collective-permute-done.5.xt_ref, bf16[512,512]{1,0:T(8,128)(2,1)S(1)} %get-tuple-element.32.qo, bf16[512,512]{1,0:T(8,128)(2,1)S(1)} %get-tuple-element.31.qt, ...), custom_call_target="tpu_custom_call" | custom-call | flops 10737418240 | bytes 9437184 | tf_op jit(solution)/shard_map/attend/pallas_call | solution.py:52
  265.2 19.5 %attend.3.co_ref = bf16[4,512,512]{2,1,0:T(8,128)(2,1)S(1)} custom-call(bf16[4,512,512]{2,1,0:T(8,128)(2,1)S(1)} %get-tuple-element.22.xo_ref, bf16[4,512,512]{2,1,0:T(8,128)(2,1)} %collective-permute-done.7.xt_ref, bf16[512,512]{1,0:T(8,128)(2,1)S(1)} %get-tuple-element.32.qo, bf16[512,512]{1,0:T(8,128)(2,1)S(1)} %get-tuple-element.31.qt, ...), custom_call_target="tpu_custom_call" | custom-call | flops 10737418240 | bytes 9437184 | tf_op jit(solution)/shard_map/attend/pallas_call | solution.py:52
  285.3 1.4 copy-done.10
  286.8 1.4 copy-done.17
  288.2 8.1 %finish.2 = bf16[4,500,512]{2,1,0:T(8,128)(2,1)S(1)} custom-call(bf16[4,512,512]{2,1,0:T(8,128)(2,1)} %get-tuple-element.21.xo_ref, bf16[4,512,512]{2,1,0:T(8,128)(2,1)} %collective-permute-done.5.xt_ref, bf16[4,512,512]{2,1,0:T(8,128)(2,1)} %copy-done, bf16[4,512,512]{2,1,0:T(8,128)(2,1)} %copy-done.17, bf16[512,512]{1,0:T(8,128)(2,1)S(1)} %get-tuple-element.26.oo, ...), custom_call_target="tpu_custom_call" | custom-call | flops 4294967296 | bytes 12582912 | tf_op jit(solution)/shard_map/finish/pallas_call | solution.py:84
  296.4 1.3 copy-done.18
  297.7 8.0 %finish.3 = bf16[4,500,512]{2,1,0:T(8,128)(2,1)S(1)} custom-call(bf16[4,512,512]{2,1,0:T(8,128)(2,1)S(1)} %get-tuple-element.22.xo_ref, bf16[4,512,512]{2,1,0:T(8,128)(2,1)} %collective-permute-done.7.xt_ref, bf16[4,512,512]{2,1,0:T(8,128)(2,1)} %copy-done.1, bf16[4,512,512]{2,1,0:T(8,128)(2,1)} %copy-done.18, bf16[512,512]{1,0:T(8,128)(2,1)S(1)} %get-tuple-element.26.oo, ...), custom_call_target="tpu_custom_call" | custom-call | flops 4294967296 | bytes 12582912 | tf_op jit(solution)/shard_map/finish/pallas_call | solution.py:84
  306.1 3.4 %copy.16 = bf16[8,500,512]{2,0,1:T(8,128)(2,1)} copy(bf16[8,500,512]{2,1,0:T(8,128)(2,1)S(1)} %pad_maximum_fusion) | data formatting | bytes 8192000 | tf_op jit(solution)/shard_map/concatenate | solution.py:213
  (97 shorter events, 10.1 us)
Async XLA Ops:
  0.8 10.1 %copy-start.16 = (s32[8,500]{1,0:T(8,128)S(1)}, s32[8,500]{1,0:T(8,128)}, u32[]{:S(2)}) copy-start(s32[8,500]{1,0:T(8,128)} %param.11) | copy-start | bytes 48004
  0.8 19.9 %collective-permute-start = (bf16[64,512]{1,0:T(8,128)(2,1)S(1)}, bf16[64,512]{1,0:T(8,128)(2,1)S(1)}, u32[]{:S(2)}, u32[]{:S(2)}) collective-permute-start(bf16[64,512]{1,0:T(8,128)(2,1)S(1)} %slice.63), channel_id=1, source_target_pairs={{0,16},{2,18},{4,20},{6,22},{8,24},{10,26},{12,28},{14,30},{16,0},... | collective-permute-start | bytes 196616 | tf_op jit(solution)/shard_map/ppermute | solution.py:143
  2.0 44.1 %collective-permute-start.2 = (bf16[640,512]{1,0:T(8,128)(2,1)S(1)}, bf16[640,512]{1,0:T(8,128)(2,1)}, u32[]{:S(2)}, u32[]{:S(2)}) collective-permute-start(bf16[640,512]{1,0:T(8,128)(2,1)S(1)} %slice.71), channel_id=1, source_target_pairs={{0,16},{2,18},{4,20},{6,22},{8,24},{10,26},{12,28},{14,30},{16,0},... | collective-permute-start | bytes 1966088 | tf_op jit(solution)/shard_map/ppermute | solution.py:143
  11.0 16.6 %copy-start.4 = (bf16[2048,512]{1,0:T(8,128)(2,1)S(1)}, bf16[2048,512]{1,0:T(8,128)(2,1)}, u32[]{:S(2)}) copy-start(bf16[2048,512]{1,0:T(8,128)(2,1)} %param.12) | copy-start | bytes 6291460
  11.2 11.8 %copy-start.11 = (s32[4000]{0:T(1024)}, s32[4000]{0:T(1024)S(1)}, u32[]{:S(2)}) copy-start(s32[4000]{0:T(1024)S(1)} %get-tuple-element.13) | copy-start | bytes 48004
  20.7 2.2 copy-start.13
  23.0 9.1 %all-to-all-start = ((s32[8,1,1008]{2,1,0:T(1,128)}), s32[8,1,1008]{2,1,0:T(1,128)S(1)}, u32[]{:S(2)}, u32[]{:S(2)}) async-start(s32[8,1,1008]{2,1,0:T(1,128)} %all_to_all.14), calls=%async_computation | async-start | bytes 65536 | tf_op jit(solution)/shard_map/all_to_all | solution.py:138
  27.6 36.7 %collective-permute-start.1 = (bf16[512,512]{1,0:T(8,128)(2,1)S(1)}, bf16[512,512]{1,0:T(8,128)(2,1)}, u32[]{:S(2)}, u32[]{:S(2)}) collective-permute-start(bf16[512,512]{1,0:T(8,128)(2,1)S(1)} %slice.70), channel_id=1, source_target_pairs={{0,16},{2,18},{4,20},{6,22},{8,24},{10,26},{12,28},{14,30},{16,0},... | collective-permute-start | bytes 1572872 | tf_op jit(solution)/shard_map/ppermute | solution.py:143
  64.3 5.8 %copy-start.15 = (s32[8,504]{1,0:T(8,128)S(1)}, s32[8,504]{1,0:T(8,128)}, u32[]{:S(2)}) copy-start(s32[8,504]{1,0:T(8,128)} %get-tuple-element.33) | copy-start | bytes 48388
  64.3 66.1 %copy-start.14 = (bf16[64,512]{1,0:T(8,128)(2,1)S(1)}, bf16[64,512]{1,0:T(8,128)(2,1)}, u32[]{:S(2)}) copy-start(bf16[64,512]{1,0:T(8,128)(2,1)} %copy-done.13) | copy-start | bytes 196612
  64.3 84.8 %all-to-all-start.1 = ((bf16[8,504,512]{2,1,0:T(8,128)(2,1)}), bf16[8,504,512]{2,1,0:T(8,128)(2,1)}, u32[]{:S(2)}, u32[]{:S(2)}) async-start(bf16[8,504,512]{2,1,0:T(8,128)(2,1)} %bitcast.46), calls=%async_computation.1 | async-start | bytes 8257536 | tf_op jit(solution)/shard_map/all_to_all | solution.py:138
  70.0 60.4 %collective-permute-start.4 = (bf16[832,512]{1,0:T(8,128)(2,1)}, bf16[832,512]{1,0:T(8,128)(2,1)S(1)}, u32[]{:S(2)}, u32[]{:S(2)}) collective-permute-start(bf16[832,512]{1,0:T(8,128)(2,1)} %slice.78), channel_id=1, source_target_pairs={{0,16},{2,18},{4,20},{6,22},{8,24},{10,26},{12,28},{14,30},{16,0},... | collective-permute-start | bytes 2555912 | tf_op jit(solution)/shard_map/ppermute | solution.py:163
  149.1 11.0 %copy-start.7 = (bf16[512,1024]{1,0:T(8,128)(2,1)S(1)}, bf16[512,1024]{1,0:T(8,128)(2,1)}, u32[]{:S(2)}) copy-start(bf16[512,1024]{1,0:T(8,128)(2,1)} %param.17) | copy-start | bytes 3145732
  149.1 15.9 %copy-start.12 = (s32[4000]{0:T(1024)S(1)}, s32[4000]{0:T(1024)}, u32[]{:S(2)}) copy-start(s32[4000]{0:T(1024)} %copy-done.11) | copy-start | bytes 48004
  149.1 60.7 %all-to-all-start.2 = ((bf16[8,504,512]{2,1,0:T(8,128)(2,1)}), bf16[8,504,512]{2,1,0:T(8,128)(2,1)}, u32[]{:S(2)}, u32[]{:S(2)}) async-start(bf16[8,504,512]{2,1,0:T(8,128)(2,1)} %bitcast.45), calls=%async_computation.2 | async-start | bytes 8257536 | tf_op jit(solution)/shard_map/all_to_all | solution.py:138
  160.1 5.9 %collective-permute-start.3 = (bf16[512,1024]{1,0:T(8,128)(2,1)S(1)}, bf16[512,1024]{1,0:T(8,128)(2,1)S(1)}, u32[]{:S(2)}, u32[]{:S(2)}) collective-permute-start(bf16[512,1024]{1,0:T(8,128)(2,1)S(1)} %copy-done.7), channel_id=1, source_target_pairs={{0,1},{1,0},{2,3},{3,2},{4,5},{5,4},{6,7},{7,6},{8,9},{9,8},{10,11... | collective-permute-start | bytes 3145736 | tf_op jit(solution)/shard_map/ppermute | solution.py:101
  166.0 12.3 %copy-start.9 = (bf16[512,1024]{1,0:T(8,128)(2,1)}, bf16[512,1024]{1,0:T(8,128)(2,1)S(1)}, u32[]{:S(2)}) copy-start(bf16[512,1024]{1,0:T(8,128)(2,1)S(1)} %collective-permute-done.3) | copy-start | bytes 3145732
  238.7 1.9 copy-start.5
  238.7 6.9 %collective-permute-start.5 = (bf16[4,512,512]{2,1,0:T(8,128)(2,1)}, bf16[4,512,512]{2,1,0:T(8,128)(2,1)}, u32[]{:S(2)}, u32[]{:S(2)}) collective-permute-start(bf16[4,512,512]{2,1,0:T(8,128)(2,1)} %get-tuple-element.21.xo_ref), channel_id=1, source_target_pairs={{0,1},{1,0},{2,3},{3,2},{4,5},{5,4},{6,7},{7,6},{8,9},{9,8},{10,11... | collective-permute-start | bytes 6291464 | tf_op jit(solution)/shard_map/ppermute | solution.py:101
  239.2 26.0 %collective-permute-start.7 = (bf16[4,512,512]{2,1,0:T(8,128)(2,1)S(1)}, bf16[4,512,512]{2,1,0:T(8,128)(2,1)}, u32[]{:S(2)}, u32[]{:S(2)}) collective-permute-start(bf16[4,512,512]{2,1,0:T(8,128)(2,1)S(1)} %get-tuple-element.22.xo_ref), channel_id=1, source_target_pairs={{0,1},{1,0},{2,3},{3,2},{4,5},{5,4},{6,7},{7,6},{8,9},{9,8},{10,11... | collective-permute-start | bytes 6291464 | tf_op jit(solution)/shard_map/ppermute | solution.py:101
  239.3 1.6 copy-start.6
  264.7 20.0 %copy-start = (bf16[4,512,512]{2,1,0:T(8,128)(2,1)}, bf16[4,512,512]{2,1,0:T(8,128)(2,1)S(1)}, u32[]{:S(2)}) copy-start(bf16[4,512,512]{2,1,0:T(8,128)(2,1)S(1)} %attend.2.co_ref) | copy-start | bytes 6291460
  264.7 20.5 %copy-start.8 = (bf16[512,1024]{1,0:T(8,128)(2,1)S(1)}, bf16[512,1024]{1,0:T(8,128)(2,1)}, u32[]{:S(2)}) copy-start(bf16[512,1024]{1,0:T(8,128)(2,1)} %param.17) | copy-start | bytes 3145732
  264.7 22.1 %collective-permute-start.6 = (bf16[4,512,512]{2,1,0:T(8,128)(2,1)S(1)}, bf16[4,512,512]{2,1,0:T(8,128)(2,1)S(1)}, u32[]{:S(2)}, u32[]{:S(2)}) collective-permute-start(bf16[4,512,512]{2,1,0:T(8,128)(2,1)S(1)} %attend.2.co_ref), channel_id=1, source_target_pairs={{0,1},{1,0},{2,3},{3,2},{4,5},{5,4},{6,7},{7,6},{8,9},{9,8},{10,11... | collective-permute-start | bytes 6291464 | tf_op jit(solution)/shard_map/ppermute | solution.py:101
  284.7 2.1 copy-start.1
  284.7 2.0 copy-start.10
  284.7 3.5 %copy-start.2 = (f32[512]{0:T(512)S(1)}, f32[512]{0:T(512)}, u32[]{:S(2)}) copy-start(f32[512]{0:T(512)} %param.18) | copy-start | bytes 6148
  284.8 3.5 %copy-start.3 = (f32[512]{0:T(512)S(1)}, f32[512]{0:T(512)}, u32[]{:S(2)}) copy-start(f32[512]{0:T(512)} %param.19) | copy-start | bytes 6148
  284.8 11.6 %collective-permute-start.8 = (bf16[4,512,512]{2,1,0:T(8,128)(2,1)S(1)}, bf16[4,512,512]{2,1,0:T(8,128)(2,1)S(1)}, u32[]{:S(2)}, u32[]{:S(2)}) collective-permute-start(bf16[4,512,512]{2,1,0:T(8,128)(2,1)S(1)} %attend.3.co_ref), channel_id=1, source_target_pairs={{0,1},{1,0},{2,3},{3,2},{4,5},{5,4},{6,7},{7,6},{8,9},{9,8},{10,11... | collective-permute-start | bytes 6291464 | tf_op jit(solution)/shard_map/ppermute | solution.py:101
  286.8 1.4 copy-start.17
  296.4 1.3 copy-start.18

commit v4 on v3

--- a/solution.py
+++ b/solution.py
@@ -11,7 +11,6 @@
 HEAD_DIM = 64
 PAIR = 2 * HEAD_DIM
 SPLIT = 2
-CUTS = (0, 1, 11, 19)
 
 
 def mm(a, b):
@@ -132,25 +131,20 @@
     groups = [list(range(half)), list(range(half, n_leaf))]
     side = lax.axis_index("leaf") // half
     mirror = [(i, (i + half) % n_leaf) for i in range(n_leaf)]
-    cuts = [table.shape[0] * c // 32 for c in CUTS]
 
     def exchange(a):
         return lax.all_to_all(
             a, "leaf", split_axis=0, concat_axis=0, tiled=True, axis_index_groups=groups
         )
 
-    def mirrored(piece, beside):
-        moved = lax.ppermute(table[cuts[piece] : cuts[piece + 1]], "leaf", mirror)
-        return lax.optimization_barrier((moved, beside))
-
+    far_table = lax.ppermute(table, "leaf", mirror)
     owner = cand_owner.reshape(total)
     onehot, rank = rank_candidates(owner, n_leaf)
-    far_a, rank = mirrored(0, rank)
     requests = place_requests(onehot, rank, cand_row.reshape(total), capacity)
     sides = requests.reshape(2, half, capacity)
     near = lax.dynamic_index_in_dim(sides, side, 0, keepdims=False)
     far = lax.dynamic_index_in_dim(sides, 1 - side, 0, keepdims=False)
-    far_b, asked = mirrored(1, exchange(jnp.concatenate([near, far], axis=1)))
+    asked = exchange(jnp.concatenate([near, far], axis=1))
 
     def find(block, places):
         return block.at[places.reshape(half * capacity)].get(mode="promise_in_bounds")
@@ -158,10 +152,8 @@
     def send(found):
         return exchange(found.reshape(half, capacity, cols)).reshape(half * capacity, cols)
 
-    far_c, found = mirrored(2, find(table, asked[:, :capacity]))
+    far_table, found = lax.optimization_barrier((far_table, find(table, asked[:, :capacity])))
     fetched_near = send(found)
-    far_d = lax.ppermute(table[cuts[3] :], "leaf", mirror)
-    far_table = jnp.concatenate([far_a, far_b, far_c, far_d], axis=0)
     fetched_far = send(find(far_table, asked[:, capacity:]))
 
     def rows_of(w, start):
@@ -182,14 +174,17 @@
     shift = jnp.pad(position, ((0, padded - length), (0, 0)), mode="edge").astype(jnp.float32)
     part = users // SPLIT
     mine, theirs, context, context_other = [], [], [], []
+    places = target.reshape(users * padded)
+
+    def pick(fetched, some):
+        picked = fetched.at[some].get(mode="promise_in_bounds")
+        return picked.reshape(-1, padded, cols)
+
+    fetched_far, every_near = lax.optimization_barrier((fetched_far, pick(fetched_near, places)))
     for index in range(SPLIT):
         some = slice(index * part, (index + 1) * part)
-        places = target[some].reshape(part * padded)
-        rows_near, rows_far = (
-            f.at[places].get(mode="promise_in_bounds").reshape(part, padded, cols)
-            for f in (fetched_near, fetched_far)
-        )
-        rows = jnp.where(is_near[some][:, :, None], rows_near, rows_far)
+        rows_far = pick(fetched_far, target[some].reshape(part * padded))
+        rows = jnp.where(is_near[some][:, :, None], every_near[some], rows_far)
         x = (rows.astype(jnp.float32) + shift[None]).astype(jnp.bfloat16)
         mine.append(x)
         theirs.append(swap(x))

time: 316 us -> 308 us (0.975)
  blocking collectives: 0 us -> 36.5 us
  waiting for transfers between devices: 112 us -> 89.3 us
  starting transfers between devices: 27.4 us -> 14.3 us
  local copies, waits for them, and re-layouts: 98.9 us -> 93.1 us
    ppermute x4 -> x1, waiting for transfers between devices: 83.7 us -> 31 us  [shards(): far_table = lax.ppermute(table, 'leaf', mirror)]
    all_to_all x0 -> x1, blocking collectives: none -> 36.5 us  [exchange(): lax.all_to_all(a, 'leaf', split_axis=0, concat_axis=0, tiled=True, axis_i...]
    all_to_all x3 -> x2, waiting for transfers between devices: 23.9 us -> 53.7 us  [exchange(): lax.all_to_all(a, 'leaf', split_axis=0, concat_axis=0, tiled=True, axis_i...]
    all_to_all x3 -> x2, starting transfers between devices: 20.3 us -> 10.6 us  [exchange(): lax.all_to_all(a, 'leaf', split_axis=0, concat_axis=0, tiled=True, axis_i...]
    gather x4 -> x3, local copies, waits for them, and re-layouts: 48.1 us -> 44.4 us  [pick(): picked = fetched.at[some].get(mode='promise_in_bounds')]
  transfers between devices with their start and end apart: 12 -> 8, of which waited for: 6 -> 4; matrix products, arithmetic and copies ran while one was open for 25% -> 23% of each run, Pallas kernels for 15% -> 15%
where the time goes in v4:
time: 308 us; the launch traced here: 303 us
  local copies, waits for them, and re-layouts  93.1 us (30%)
  waiting for transfers between devices  89.3 us (29%)
  Pallas kernels  54.7 us (18%)
  blocking collectives  36.5 us (12%)
  starting transfers between devices  14.3 us (5%)
  other arithmetic  13 us (4%)
    all_to_all x2, waiting for transfers between devices, exchange(): lax.all_to_all(a, 'leaf', split_axis=0, concat_axis=0, tiled=True, axis_i...  53.7 us
    gather x3, local copies, waits for them, and re-layouts, pick(): picked = fetched.at[some].get(mode='promise_in_bounds')  44.4 us
    pallas_call x2, Pallas kernels, attend(): pl.pallas_call(functools.partial(attend_kernel, length), grid=(users,), o...  38.6 us
    gather x2, local copies, waits for them, and re-layouts, find(): block.at[places.reshape(half * capacity)].get(mode='promise_in_bounds')  36.6 us
    all_to_all x1, blocking collectives, exchange(): lax.all_to_all(a, 'leaf', split_axis=0, concat_axis=0, tiled=True, axis_i...  36.5 us
    ppermute x1, waiting for transfers between devices, shards(): far_table = lax.ppermute(table, 'leaf', mirror)  31 us
    pallas_call x2, Pallas kernels, finish(): pl.pallas_call(functools.partial(finish_kernel, length), grid=(users,), o...  16.1 us
    all_to_all x2, starting transfers between devices, exchange(): lax.all_to_all(a, 'leaf', split_axis=0, concat_axis=0, tiled=True, axis_i...  10.6 us
  transfers between devices with their start and end apart: 8, of which 4 were waited for; matrix products, arithmetic and copies ran while one was open for 23% of the time, Pallas kernels for 15%

profile of v4, /device:TPU:29, one launch (start us, length us, event | category | flops | bytes accessed | tf_op | source)
XLA Modules:
  0.0 302.8 jit_solution(17633298530905302020)
XLA Ops:
  0.1 0.8 broadcast_multiply_fusion
  1.0 4.6 %reduce-window.6 = s32[16,32,128]{2,1,0:T(8,128)S(1)} reduce-window(s32[16,32,128]{2,1,0:T(8,128)S(1)} %bitcast.61, s32[]{:T(128)} %constant.74.clone.1), window={size=1x1x128 pad=0_0x0_0x127_0}, to_apply=%region_0.1 | reduce-window | flops 8323072 | bytes 524292 | tf_op jit(solution)/shard_map/reduce-window
  5.7 0.5 slice_reduce_fusion
  6.9 1.5 fusion.2
  8.5 36.5 %all_to_all.22 = s32[8,1,1008]{2,1,0:T(1,128)S(1)} all-to-all(s32[8,1,1008]{2,1,0:T(1,128)S(1)} %all_to_all.14), channel_id=1, replica_groups={{0,2,4,6,8,10,12,14},{16,18,20,22,24,26,28,30},{1,3,5,7,9,11,13,15},{17..., dimensions={0} | all-to-all | bytes 64512 | tf_op jit(solution)/shard_map/all_to_all | solution.py:136
  45.2 17.3 %gather_fusion = bf16[4032,512]{1,0:T(8,128)(2,1)} fusion(bf16[2048,512]{1,0:T(8,128)(2,1)S(1)} %copy-done.4, s32[4096]{0:T(1024)S(1)} %pad_clamp_fusion.1), kind=kCustom, calls=%fused_computation | custom fusion | bytes 8273664 | tf_op jit(solution)/shard_map/gather | solution.py:150
  62.6 31.0 %collective-permute-done = bf16[2048,512]{1,0:T(8,128)(2,1)} collective-permute-done((bf16[2048,512]{1,0:T(8,128)(2,1)}, bf16[2048,512]{1,0:T(8,128)(2,1)}, u32[]{:S(2)}, u32[]{:S(2)}) %collective-permute-start) | collective-permute-done | bytes 2097184 | tf_op jit(solution)/shard_map/ppermute | solution.py:140
  93.6 4.6 %all-to-all-start.2 = ((bf16[8,504,512]{2,1,0:T(8,128)(2,1)}), bf16[8,504,512]{2,1,0:T(8,128)(2,1)}, u32[]{:S(2)}, u32[]{:S(2)}) async-start(bf16[8,504,512]{2,1,0:T(8,128)(2,1)} %bitcast.58), calls=%async_computation.2 | async-start | bytes 8257536 | tf_op jit(solution)/shard_map/all_to_all | solution.py:136
  98.3 19.3 %gather_fusion.1 = bf16[4032,512]{1,0:T(8,128)(2,1)} fusion(bf16[2048,512]{1,0:T(8,128)(2,1)} %collective-permute-done, s32[4096]{0:T(1024)S(1)} %pad_clamp_fusion), kind=kCustom, calls=%fused_computation.1 | custom fusion | bytes 8273664 | tf_op jit(solution)/shard_map/gather | solution.py:150
  117.6 30.4 %all-to-all-done.2 = bf16[8,504,512]{2,1,0:T(8,128)(2,1)} async-done(((bf16[8,504,512]{2,1,0:T(8,128)(2,1)}), bf16[8,504,512]{2,1,0:T(8,128)(2,1)}, u32[]{:S(2)}, u32[]{:S(2)}) %all-to-all-start.2) | async-done | bytes 4128800 | tf_op jit(solution)/shard_map/all_to_all | solution.py:136
  148.0 6.1 %all-to-all-start.1 = ((bf16[8,504,512]{2,1,0:T(8,128)(2,1)}), bf16[8,504,512]{2,1,0:T(8,128)(2,1)}, u32[]{:S(2)}, u32[]{:S(2)}) async-start(bf16[8,504,512]{2,1,0:T(8,128)(2,1)} %bitcast.57), calls=%async_computation.1 | async-start | bytes 8257536 | tf_op jit(solution)/shard_map/all_to_all | solution.py:136
  154.1 2.2 collective-permute-start.1
  157.2 0.7 slice_reduce_fusion.3
  158.0 1.2 maximum_convert_fusion
  159.3 20.5 %gather_fusion.2 = bf16[4096,512]{1,0:T(8,128)(2,1)} fusion(bf16[4032,512]{1,0:T(8,128)(2,1)} %bitcast.8, s32[4096]{0:T(1024)S(1)} %broadcast_clamp_fusion), kind=kCustom, calls=%fused_computation.2 | custom fusion | bytes 8404992 | tf_op jit(solution)/shard_map/gather | solution.py:180
  179.8 23.3 %all-to-all-done.1 = bf16[8,504,512]{2,1,0:T(8,128)(2,1)} async-done(((bf16[8,504,512]{2,1,0:T(8,128)(2,1)}), bf16[8,504,512]{2,1,0:T(8,128)(2,1)}, u32[]{:S(2)}, u32[]{:S(2)}) %all-to-all-start.1) | async-done | bytes 4128800 | tf_op jit(solution)/shard_map/all_to_all | solution.py:136
  203.1 12.0 %gather_fusion.4 = bf16[2048,512]{1,0:T(8,128)(2,1)} fusion(bf16[4032,512]{1,0:T(8,128)(2,1)} %bitcast.6, s32[2048]{0:T(1024)S(1)} %broadcast_clamp_fusion.1), kind=kCustom, calls=%fused_computation.4 | custom fusion | bytes 4202496 | tf_op jit(solution)/shard_map/gather | solution.py:180
  215.0 12.0 %gather_fusion.3 = bf16[2048,512]{1,0:T(8,128)(2,1)} fusion(bf16[4032,512]{1,0:T(8,128)(2,1)} %bitcast.6, s32[2048]{0:T(1024)S(1)} %broadcast_clamp_fusion.2), kind=kCustom, calls=%fused_computation.3 | custom fusion | bytes 4202496 | tf_op jit(solution)/shard_map/gather | solution.py:180
  227.0 5.1 %add_convert_fusion.1 = (bf16[4,512,512]{2,1,0:T(8,128)(2,1)}, bf16[4,512,512]{2,1,0:T(8,128)(2,1)S(1)}) fusion(f32[512,512]{1,0:T(8,128)S(1)} %maximum_convert_fusion, bf16[4,512,512]{2,1,0:T(8,128)(2,1)} %bitcast.60, bf16[8,512,512]{2,1,0:T(8,128)(2,1)} %bitcast.56, pred[4,512]{1,0:T(4,128)(4,1)S(1)} %get-tuple-element.42, ...), kind=kLoop, calls=%fused_computation.8 | loop fusion | flops 8388608 | bytes 13635584 | tf_op jit(solution)/shard_map/convert_element_type | solution.py:188
  232.1 0.5 collective-permute-start.2
  232.7 1.4 constant_dynamic-slice_fusion.8
  234.5 4.5 %collective-permute-done.2.xt_ref = bf16[4,512,512]{2,1,0:T(8,128)(2,1)} collective-permute-done((bf16[4,512,512]{2,1,0:T(8,128)(2,1)}, bf16[4,512,512]{2,1,0:T(8,128)(2,1)}, u32[]{:S(2)}, u32[]{:S(2)}) %collective-permute-start.2) | collective-permute-done | bytes 2097184 | tf_op jit(solution)/shard_map/ppermute | solution.py:100
  239.0 19.1 %attend.2.co_ref = bf16[4,512,512]{2,1,0:T(8,128)(2,1)S(1)} custom-call(bf16[4,512,512]{2,1,0:T(8,128)(2,1)} %get-tuple-element.17.xo_ref, bf16[4,512,512]{2,1,0:T(8,128)(2,1)} %collective-permute-done.2.xt_ref, bf16[512,512]{1,0:T(8,128)(2,1)S(1)} %get-tuple-element.28.qo, bf16[512,512]{1,0:T(8,128)(2,1)S(1)} %get-tuple-element.27.qt, ...), custom_call_target="tpu_custom_call" | custom-call | flops 10737418240 | bytes 9437184 | tf_op jit(solution)/shard_map/attend/pallas_call | solution.py:51
  258.1 0.4 collective-permute-start.3
  258.6 19.5 %attend.3.co_ref = bf16[4,512,512]{2,1,0:T(8,128)(2,1)S(1)} custom-call(bf16[4,512,512]{2,1,0:T(8,128)(2,1)S(1)} %get-tuple-element.18.xo_ref, bf16[4,512,512]{2,1,0:T(8,128)(2,1)} %collective-permute-done.4.xt_ref, bf16[512,512]{1,0:T(8,128)(2,1)S(1)} %get-tuple-element.28.qo, bf16[512,512]{1,0:T(8,128)(2,1)S(1)} %get-tuple-element.27.qt, ...), custom_call_target="tpu_custom_call" | custom-call | flops 10737418240 | bytes 9437184 | tf_op jit(solution)/shard_map/attend/pallas_call | solution.py:51
  278.2 0.4 collective-permute-start.5
  278.7 1.4 copy-done.10
  280.2 1.4 copy-done.12
  281.6 8.1 %finish.2 = bf16[4,500,512]{2,1,0:T(8,128)(2,1)S(1)} custom-call(bf16[4,512,512]{2,1,0:T(8,128)(2,1)} %get-tuple-element.17.xo_ref, bf16[4,512,512]{2,1,0:T(8,128)(2,1)} %collective-permute-done.2.xt_ref, bf16[4,512,512]{2,1,0:T(8,128)(2,1)} %copy-done, bf16[4,512,512]{2,1,0:T(8,128)(2,1)} %copy-done.12, bf16[512,512]{1,0:T(8,128)(2,1)S(1)} %get-tuple-element.22.oo, ...), custom_call_target="tpu_custom_call" | custom-call | flops 4294967296 | bytes 12582912 | tf_op jit(solution)/shard_map/finish/pallas_call | solution.py:83
  289.8 1.3 copy-done.13
  291.1 8.0 %finish.3 = bf16[4,500,512]{2,1,0:T(8,128)(2,1)S(1)} custom-call(bf16[4,512,512]{2,1,0:T(8,128)(2,1)S(1)} %get-tuple-element.18.xo_ref, bf16[4,512,512]{2,1,0:T(8,128)(2,1)} %collective-permute-done.4.xt_ref, bf16[4,512,512]{2,1,0:T(8,128)(2,1)} %copy-done.1, bf16[4,512,512]{2,1,0:T(8,128)(2,1)} %copy-done.13, bf16[512,512]{1,0:T(8,128)(2,1)S(1)} %get-tuple-element.22.oo, ...), custom_call_target="tpu_custom_call" | custom-call | flops 4294967296 | bytes 12582912 | tf_op jit(solution)/shard_map/finish/pallas_call | solution.py:83
  299.4 3.4 %copy.13 = bf16[8,500,512]{2,0,1:T(8,128)(2,1)} copy(bf16[8,500,512]{2,1,0:T(8,128)(2,1)S(1)} %pad_maximum_fusion) | data formatting | bytes 8192000 | tf_op jit(solution)/shard_map/concatenate | solution.py:208
  (77 shorter events, 3.5 us)
Async XLA Ops:
  0.0 6.6 %copy-start.11 = (s32[8,500]{1,0:T(8,128)S(1)}, s32[8,500]{1,0:T(8,128)}, u32[]{:S(2)}) copy-start(s32[8,500]{1,0:T(8,128)} %param.11) | copy-start | bytes 48004
  0.0 93.6 %collective-permute-start = (bf16[2048,512]{1,0:T(8,128)(2,1)}, bf16[2048,512]{1,0:T(8,128)(2,1)}, u32[]{:S(2)}, u32[]{:S(2)}) collective-permute-start(bf16[2048,512]{1,0:T(8,128)(2,1)} %param.12), channel_id=1, source_target_pairs={{0,16},{2,18},{4,20},{6,22},{8,24},{10,26},{12,28},{14,30},{16,0},... | collective-permute-start | bytes 6291464 | tf_op jit(solution)/shard_map/ppermute | solution.py:140
  6.6 38.6 %copy-start.4 = (bf16[2048,512]{1,0:T(8,128)(2,1)S(1)}, bf16[2048,512]{1,0:T(8,128)(2,1)}, u32[]{:S(2)}) copy-start(bf16[2048,512]{1,0:T(8,128)(2,1)} %param.12) | copy-start | bytes 6291460
  93.6 54.4 %all-to-all-start.2 = ((bf16[8,504,512]{2,1,0:T(8,128)(2,1)}), bf16[8,504,512]{2,1,0:T(8,128)(2,1)}, u32[]{:S(2)}, u32[]{:S(2)}) async-start(bf16[8,504,512]{2,1,0:T(8,128)(2,1)} %bitcast.58), calls=%async_computation.2 | async-start | bytes 8257536 | tf_op jit(solution)/shard_map/all_to_all | solution.py:136
  148.0 6.1 %copy-start.7 = (bf16[512,1024]{1,0:T(8,128)(2,1)S(1)}, bf16[512,1024]{1,0:T(8,128)(2,1)}, u32[]{:S(2)}) copy-start(bf16[512,1024]{1,0:T(8,128)(2,1)} %param.17) | copy-start | bytes 3145732
  148.0 55.0 %all-to-all-start.1 = ((bf16[8,504,512]{2,1,0:T(8,128)(2,1)}), bf16[8,504,512]{2,1,0:T(8,128)(2,1)}, u32[]{:S(2)}, u32[]{:S(2)}) async-start(bf16[8,504,512]{2,1,0:T(8,128)(2,1)} %bitcast.57), calls=%async_computation.1 | async-start | bytes 8257536 | tf_op jit(solution)/shard_map/all_to_all | solution.py:136
  154.1 5.1 %collective-permute-start.1 = (bf16[512,1024]{1,0:T(8,128)(2,1)S(1)}, bf16[512,1024]{1,0:T(8,128)(2,1)S(1)}, u32[]{:S(2)}, u32[]{:S(2)}) collective-permute-start(bf16[512,1024]{1,0:T(8,128)(2,1)S(1)} %copy-done.7), channel_id=1, source_target_pairs={{0,1},{1,0},{2,3},{3,2},{4,5},{5,4},{6,7},{7,6},{8,9},{9,8},{10,11... | collective-permute-start | bytes 3145736 | tf_op jit(solution)/shard_map/ppermute | solution.py:100
  159.2 20.5 %copy-start.9 = (bf16[512,1024]{1,0:T(8,128)(2,1)}, bf16[512,1024]{1,0:T(8,128)(2,1)S(1)}, u32[]{:S(2)}) copy-start(bf16[512,1024]{1,0:T(8,128)(2,1)S(1)} %collective-permute-done.1) | copy-start | bytes 3145732
  232.1 1.9 copy-start.5
  232.1 6.9 %collective-permute-start.2 = (bf16[4,512,512]{2,1,0:T(8,128)(2,1)}, bf16[4,512,512]{2,1,0:T(8,128)(2,1)}, u32[]{:S(2)}, u32[]{:S(2)}) collective-permute-start(bf16[4,512,512]{2,1,0:T(8,128)(2,1)} %get-tuple-element.17.xo_ref), channel_id=1, source_target_pairs={{0,1},{1,0},{2,3},{3,2},{4,5},{5,4},{6,7},{7,6},{8,9},{9,8},{10,11... | collective-permute-start | bytes 6291464 | tf_op jit(solution)/shard_map/ppermute | solution.py:100
  232.6 26.0 %collective-permute-start.4 = (bf16[4,512,512]{2,1,0:T(8,128)(2,1)S(1)}, bf16[4,512,512]{2,1,0:T(8,128)(2,1)}, u32[]{:S(2)}, u32[]{:S(2)}) collective-permute-start(bf16[4,512,512]{2,1,0:T(8,128)(2,1)S(1)} %get-tuple-element.18.xo_ref), channel_id=1, source_target_pairs={{0,1},{1,0},{2,3},{3,2},{4,5},{5,4},{6,7},{7,6},{8,9},{9,8},{10,11... | collective-permute-start | bytes 6291464 | tf_op jit(solution)/shard_map/ppermute | solution.py:100
  232.7 1.6 copy-start.6
  258.1 20.0 %copy-start = (bf16[4,512,512]{2,1,0:T(8,128)(2,1)}, bf16[4,512,512]{2,1,0:T(8,128)(2,1)S(1)}, u32[]{:S(2)}) copy-start(bf16[4,512,512]{2,1,0:T(8,128)(2,1)S(1)} %attend.2.co_ref) | copy-start | bytes 6291460
  258.1 20.5 %copy-start.8 = (bf16[512,1024]{1,0:T(8,128)(2,1)S(1)}, bf16[512,1024]{1,0:T(8,128)(2,1)}, u32[]{:S(2)}) copy-start(bf16[512,1024]{1,0:T(8,128)(2,1)} %param.17) | copy-start | bytes 3145732
  258.1 22.1 %collective-permute-start.3 = (bf16[4,512,512]{2,1,0:T(8,128)(2,1)S(1)}, bf16[4,512,512]{2,1,0:T(8,128)(2,1)S(1)}, u32[]{:S(2)}, u32[]{:S(2)}) collective-permute-start(bf16[4,512,512]{2,1,0:T(8,128)(2,1)S(1)} %attend.2.co_ref), channel_id=1, source_target_pairs={{0,1},{1,0},{2,3},{3,2},{4,5},{5,4},{6,7},{7,6},{8,9},{9,8},{10,11... | collective-permute-start | bytes 6291464 | tf_op jit(solution)/shard_map/ppermute | solution.py:100
  278.1 2.1 copy-start.1
  278.1 2.0 copy-start.10
  278.1 3.5 %copy-start.2 = (f32[512]{0:T(512)S(1)}, f32[512]{0:T(512)}, u32[]{:S(2)}) copy-start(f32[512]{0:T(512)} %param.18) | copy-start | bytes 6148
  278.1 3.5 %copy-start.3 = (f32[512]{0:T(512)S(1)}, f32[512]{0:T(512)}, u32[]{:S(2)}) copy-start(f32[512]{0:T(512)} %param.19) | copy-start | bytes 6148
  278.2 11.6 %collective-permute-start.5 = (bf16[4,512,512]{2,1,0:T(8,128)(2,1)S(1)}, bf16[4,512,512]{2,1,0:T(8,128)(2,1)S(1)}, u32[]{:S(2)}, u32[]{:S(2)}) collective-permute-start(bf16[4,512,512]{2,1,0:T(8,128)(2,1)S(1)} %attend.3.co_ref), channel_id=1, source_target_pairs={{0,1},{1,0},{2,3},{3,2},{4,5},{5,4},{6,7},{7,6},{8,9},{9,8},{10,11... | collective-permute-start | bytes 6291464 | tf_op jit(solution)/shard_map/ppermute | solution.py:100
  280.2 1.4 copy-start.12
  289.8 1.3 copy-start.13
